TPU v7x, 128 devices: a whole 4x4x4 slice. The times are simulated.
128 devices in a mesh: ex: 16 (over z, y), bf: 8 (over x, core).
Axes of the slice: x: 4, y: 4, z: 4, core: 2. Of those that a mesh axis runs over, the one named last changes fastest.
Arguments:
- gradients: float32 [16, 16, 262144], P('ex', None, 'bf'), may hold values from -6 to 6
- moment_one: float32 [4194304], P(('ex', 'bf')), may hold values from -0.6 to 0.6
- moment_two: float32 [4194304], P(('ex', 'bf')), may hold values from 0.0025 to 0.04
- rademacher: int32 [4194304], P(('ex', 'bf')), may hold values from -1 to 1, as said below
- sample_rows: int32 [8192], replicated, may hold values from 0 to 4194303
- pool_order: int32 [16], replicated, may hold values from 0 to 15, each once
Outputs:
- sketch: float32 [16, 8192], P('ex', 'bf')
Inputs may be any that keep to these rules, and one draw needn't show every extreme that they name: `rademacher`: every entry is +1 or -1, never 0. `pool_order`: each of the 16 pool numbers occurs once.
All inputs are finite; a program needn't handle non-finite values.
Results may differ from a plain program's by a relative error of at most 0.0001.
Values sent between devices are 32-bit elements; how exact they have to be, the bound alone decides.
A program may use at most 64 MiB of HBM per device.

v0:
```python
import jax
import jax.numpy as jnp
from jax import lax
from jax.sharding import PartitionSpec as P

BETA_ONE = 0.9
BETA_TWO = 0.999
HIGHEST = lax.Precision.HIGHEST


def partner_2(value, axis, bit):
    return lax.ppermute(value, axis, [(i, i ^ 1 << bit) for i in range(lax.axis_size(axis))])


def bit_parity(values, width_bits):
    counted = jnp.zeros_like(values)
    for position in range(width_bits):
        counted = counted + jnp.bitwise_and(jnp.right_shift(values, position), 1)
    return jnp.bitwise_and(counted, 1)


def hadamard_matrix(matrix_order):
    indices = jnp.arange(matrix_order, dtype=jnp.int32)
    parity = bit_parity(
        jnp.bitwise_and(indices[:, None], indices[None, :]), max(matrix_order.bit_length() - 1, 1)
    )
    return (1 - 2 * parity).astype(jnp.float32)


def adam_feature(gradient, moment_one, moment_two, sign_flip):
    moment_new = BETA_ONE * moment_one + (1.0 - BETA_ONE) * gradient
    second_new = BETA_TWO * moment_two + (1.0 - BETA_TWO) * gradient * gradient
    return sign_flip * moment_new * lax.rsqrt(second_new)


def count_bits(number):
    return number.bit_length() - 1


def local_hadamard(values):
    length = values.shape[-1]
    left_size = 2 ** (count_bits(length) // 2)
    right_size = length // left_size
    shaped = values.reshape((-1, left_size, right_size))
    shaped = jnp.einsum("nab,bc->nac", shaped, hadamard_matrix(right_size), precision=HIGHEST)
    shaped = jnp.matmul(hadamard_matrix(left_size), shaped, precision=HIGHEST)
    return shaped.reshape(values.shape)


def per_device(gradients, moment_one, moment_two, rademacher, sample_rows, pool_order):
    ex_count = lax.axis_size("ex")
    bf_count = lax.axis_size("bf")
    ex_index = lax.axis_index("ex")
    bf_index = lax.axis_index("bf")
    block_len = moment_one.shape[0]
    per_dev = gradients.shape[0]
    examples = per_dev * ex_count
    scale_out = float(block_len * ex_count * bf_count) ** (-0.5)
    sample_block = sample_rows // block_len
    sample_local = sample_rows % block_len
    sign_flip = rademacher.astype(jnp.float32)
    order_matrix = (pool_order[None, :] == jnp.arange(examples, dtype=jnp.int32)[:, None]).astype(
        jnp.float32
    )
    regrouped = lax.all_to_all(gradients, "ex", split_axis=1, concat_axis=0, tiled=True).reshape(
        examples, block_len
    )
    feature = adam_feature(regrouped, moment_one, moment_two, sign_flip)
    transformed = local_hadamard(feature)
    my_block = ex_index * bf_count + bf_index
    for position in range(count_bits(ex_count)):
        partner = partner_2(transformed, "ex", position)
        upper_bit = jnp.bitwise_and(jnp.right_shift(ex_index, position), 1)
        own_sign = (1 - 2 * upper_bit).astype(jnp.float32)
        transformed = partner + own_sign * transformed
    for position in range(count_bits(bf_count)):
        partner = partner_2(transformed, "bf", position)
        upper_bit = jnp.bitwise_and(jnp.right_shift(bf_index, position), 1)
        own_sign = (1 - 2 * upper_bit).astype(jnp.float32)
        transformed = partner + own_sign * transformed
    picked = jnp.take(transformed, sample_local, axis=1)
    partial_terms = jnp.where((sample_block == my_block)[None, :], picked, 0.0)
    pooled = jnp.dot(order_matrix, partial_terms, precision=HIGHEST)
    summed = lax.psum_scatter(pooled, "ex", scatter_dimension=0, tiled=True)
    summed = lax.psum_scatter(summed, "bf", scatter_dimension=1, tiled=True)
    return summed * scale_out


def solution(mesh):
    in_specs = (P("ex", None, "bf"), P(("ex", "bf")), P(("ex", "bf")), P(("ex", "bf")), P(), P())
    out_specs = P("ex", "bf")
    return jax.shard_map(
        per_device, mesh=mesh, in_specs=in_specs, out_specs=out_specs, check_vma=False
    )
```

profile of v0, /device:TPU:1, one launch (start us, length us, event | category | flops | bytes accessed | tf_op | source)
XLA Modules:
  0.0 555.8 jit_solution(14856196350625150962)
XLA Ops:
  6.5 5.1 copy.39
  11.6 8.7 %all-to-all-start = ((f32[1,16,32768]{2,0,1:T(1,128)}), f32[1,16,32768]{2,0,1:T(1,128)S(1)}, u32[]{:S(2)}, u32[]{:S(2)}) async-start(f32[1,16,32768]{2,0,1:T(1,128)} %copy.39), calls=%async_computation | async-start | bytes 4194304 | tf_op jit(solution)/shard_map/all_to_all | solution.py:65
  20.4 0.2 all-reduce.3.cloned.1.call-start
  20.7 0.0 copy-done.4
  20.8 30.0 %all-to-all-done = f32[1,16,32768]{2,0,1:T(1,128)S(1)} async-done(((f32[1,16,32768]{2,0,1:T(1,128)}), f32[1,16,32768]{2,0,1:T(1,128)S(1)}, u32[]{:S(2)}, u32[]{:S(2)}) %all-to-all-start) | async-done | bytes 2097184 | tf_op jit(solution)/shard_map/all_to_all | solution.py:65
  50.8 7.0 %reduce = f32[16,32768]{1,0:T(8,128)} reduce(f32[1,16,32768]{2,0,1:T(1,128)S(1)} %all-to-all-done, f32[]{:T(128)} %constant.94), dimensions={0}, to_apply=%all_to_all.2.reduce_sub_computation | reduce | bytes 4194308 | tf_op jit(solution)/shard_map/all_to_all | solution.py:65
  57.8 2.2 copy.43
  60.0 0.3 fusion.9
  60.4 2.4 fusion.6
  62.7 2.0 fusion.55
  64.7 1.4 copy.44
  66.2 0.1 collective-permute-start
  66.3 1.2 copy-done.1
  67.5 43.9 %collective-permute-done = f32[16,32768]{1,0:T(8,128)} collective-permute-done((f32[16,32768]{1,0:T(8,128)S(1)}, f32[16,32768]{1,0:T(8,128)}, u32[]{:S(2)}, u32[]{:S(2)}) %collective-permute-start) | collective-permute-done | bytes 2097184 | tf_op jit(solution)/shard_map/ppermute | solution.py:12
  111.3 2.4 multiply_add_fusion.6
  113.8 2.6 collective-permute-start.1
  116.3 43.6 %collective-permute-done.1 = f32[16,32768]{1,0:T(8,128)} collective-permute-done((f32[16,32768]{1,0:T(8,128)S(1)}, f32[16,32768]{1,0:T(8,128)}, u32[]{:S(2)}, u32[]{:S(2)}) %collective-permute-start.1) | collective-permute-done | bytes 2097184 | tf_op jit(solution)/shard_map/ppermute | solution.py:12
  159.9 3.1 multiply_add_fusion.5
  163.0 1.4 collective-permute-start.2
  164.4 42.5 %collective-permute-done.2 = f32[16,32768]{1,0:T(8,128)} collective-permute-done((f32[16,32768]{1,0:T(8,128)}, f32[16,32768]{1,0:T(8,128)}, u32[]{:S(2)}, u32[]{:S(2)}) %collective-permute-start.2) | collective-permute-done | bytes 2097184 | tf_op jit(solution)/shard_map/ppermute | solution.py:12
  206.9 2.4 multiply_add_fusion.4
  209.3 0.0 copy-start
  209.3 3.7 collective-permute-start.3
  213.1 0.0 copy-done
  213.1 42.0 %collective-permute-done.3 = f32[16,32768]{1,0:T(8,128)} collective-permute-done((f32[16,32768]{1,0:T(8,128)S(1)}, f32[16,32768]{1,0:T(8,128)}, u32[]{:S(2)}, u32[]{:S(2)}) %collective-permute-start.3) | collective-permute-done | bytes 2097184 | tf_op jit(solution)/shard_map/ppermute | solution.py:12
  255.1 2.4 multiply_add_fusion.3
  257.5 4.8 collective-permute-start.4
  262.3 3.9 collective-permute-done.4
  266.2 3.1 multiply_add_fusion.2
  269.3 1.2 collective-permute-start.5
  270.6 45.9 %collective-permute-done.5 = f32[16,32768]{1,0:T(8,128)} collective-permute-done((f32[16,32768]{1,0:T(8,128)}, f32[16,32768]{1,0:T(8,128)}, u32[]{:S(2)}, u32[]{:S(2)}) %collective-permute-start.5) | collective-permute-done | bytes 2097184 | tf_op jit(solution)/shard_map/ppermute | solution.py:12
  316.5 2.4 multiply_add_fusion.1
  318.9 2.8 collective-permute-start.6
  321.8 44.7 %collective-permute-done.6 = f32[16,32768]{1,0:T(8,128)} collective-permute-done((f32[16,32768]{1,0:T(8,128)S(1)}, f32[16,32768]{1,0:T(8,128)}, u32[]{:S(2)}, u32[]{:S(2)}) %collective-permute-start.6) | collective-permute-done | bytes 2097184 | tf_op jit(solution)/shard_map/ppermute | solution.py:12
  366.5 3.1 multiply_add_fusion
  369.7 9.7 %copy.40 = f32[16,32768]{0,1:T(8,128)} copy(f32[16,32768]{1,0:T(8,128)} %multiply_add_fusion) | data formatting | bytes 4194304 | tf_op jit(solution)/shard_map/add | solution.py:80
  379.4 33.5 %gather_fusion = f32[8192,16]{1,0:T(8,128)} fusion(f32[16,32768]{0,1:T(8,128)} %copy.40, s32[8192]{0:T(1024)S(1)} %broadcast_clamp_fusion), kind=kCustom, calls=%fused_computation | custom fusion | bytes 1081344 | tf_op jit(solution)/shard_map/jit(_take)/gather | solution.py:81
  412.9 6.2 %fusion = f32[16,8192]{1,0:T(8,128)} fusion(f32[8192,16]{1,0:T(8,128)} %gather_fusion, pred[8192]{0:T(1024)(128)(4,1)S(1)} %get-tuple-element.6, pred[8192]{0:T(1024)(128)(4,1)S(1)} %get-tuple-element.5, s32[16]{0:T(128)S(1)} %copy-done.6), kind=kOutput, calls=%fused_computation.1 | convolution fusion | flops 25428224 | bytes 1065024 | tf_op jit(solution)/shard_map/dot_general | solution.py:83
  419.1 0.0 all-reduce.3.cloned.1.call-update
  419.2 0.0 reduce-scatter.4.cloned.1.call-start
  419.2 0.6 dynamic-slice
  419.8 87.3 %all-reduce.3.cloned.1.call-done = f32[16,8192]{1,0:T(8,128)} async-done(((f32[16,8192]{1,0:T(8,128)}), f32[16,8192]{1,0:T(8,128)}) %all-reduce.3.cloned.1.call-update) | async-done | bytes 524304
  507.1 1.6 constant_dynamic-slice_fusion
  508.8 2.6 copy.41
  511.4 0.0 reduce-scatter.4.cloned.1.call-update
  511.4 35.7 %reduce-scatter.4.cloned.1.call-done = f32[1024,1]{1,0:T(8,128)} async-done(((f32[8192,1]{1,0:T(8,128)}), f32[1024,1]{1,0:T(8,128)}) %reduce-scatter.4.cloned.1.call-update) | async-done | bytes 4112
  547.1 1.2 copy.42
  548.4 0.6 broadcast_multiply_fusion.2
  (20 shorter events, 0.2 us)
Async XLA Ops:
  11.6 9.0 %copy-start.2 = (f32[32768]{0:T(1024)S(1)}, f32[32768]{0:T(1024)}, u32[]{:S(2)}) copy-start(f32[32768]{0:T(1024)} %param.7) | copy-start | bytes 393220
  11.6 9.1 %copy-start.3 = (s32[32768]{0:T(1024)S(1)}, s32[32768]{0:T(1024)}, u32[]{:S(2)}) copy-start(s32[32768]{0:T(1024)} %param.9) | copy-start | bytes 393220
  11.6 9.1 %copy-start.4 = (f32[32768]{0:T(1024)S(1)}, f32[32768]{0:T(1024)}, u32[]{:S(2)}) copy-start(f32[32768]{0:T(1024)} %param.8) | copy-start | bytes 393220
  11.6 39.2 %all-to-all-start = ((f32[1,16,32768]{2,0,1:T(1,128)}), f32[1,16,32768]{2,0,1:T(1,128)S(1)}, u32[]{:S(2)}, u32[]{:S(2)}) async-start(f32[1,16,32768]{2,0,1:T(1,128)} %copy.39), calls=%async_computation | async-start | bytes 4194304 | tf_op jit(solution)/shard_map/all_to_all | solution.py:65
  20.4 486.8 %all-reduce.3.cloned.1.call-start = ((), (), s32[]{:S(2)}) async-start(), calls=%async_computation.3 | async-start | bytes 1048576
  66.1 1.3 copy-start.1
  66.2 45.2 %collective-permute-start = (f32[16,32768]{1,0:T(8,128)S(1)}, f32[16,32768]{1,0:T(8,128)}, u32[]{:S(2)}, u32[]{:S(2)}) collective-permute-start(f32[16,32768]{1,0:T(8,128)S(1)} %bitcast.22), channel_id=1, source_target_pairs={{0,8},{8,0},{16,24},{24,16},{32,40},{40,32},{48,56},{56,48},{64,72... | collective-permute-start | bytes 6291464 | tf_op jit(solution)/shard_map/ppermute | solution.py:12
  113.8 46.2 %collective-permute-start.1 = (f32[16,32768]{1,0:T(8,128)S(1)}, f32[16,32768]{1,0:T(8,128)}, u32[]{:S(2)}, u32[]{:S(2)}) collective-permute-start(f32[16,32768]{1,0:T(8,128)S(1)} %multiply_add_fusion.6), channel_id=1, source_target_pairs={{0,16},{8,24},{16,0},{24,8},{32,48},{40,56},{48,32},{56,40},{64,80... | collective-permute-start | bytes 6291464 | tf_op jit(solution)/shard_map/ppermute | solution.py:12
  163.0 43.9 %collective-permute-start.2 = (f32[16,32768]{1,0:T(8,128)}, f32[16,32768]{1,0:T(8,128)}, u32[]{:S(2)}, u32[]{:S(2)}) collective-permute-start(f32[16,32768]{1,0:T(8,128)} %multiply_add_fusion.5), channel_id=1, source_target_pairs={{0,32},{8,40},{16,48},{24,56},{32,0},{40,8},{48,16},{56,24},{64,96... | collective-permute-start | bytes 6291464 | tf_op jit(solution)/shard_map/ppermute | solution.py:12
  209.3 3.8 copy-start
  209.3 45.7 %collective-permute-start.3 = (f32[16,32768]{1,0:T(8,128)S(1)}, f32[16,32768]{1,0:T(8,128)}, u32[]{:S(2)}, u32[]{:S(2)}) collective-permute-start(f32[16,32768]{1,0:T(8,128)S(1)} %multiply_add_fusion.4), channel_id=1, source_target_pairs={{0,64},{8,72},{16,80},{24,88},{32,96},{40,104},{48,112},{56,120},{... | collective-permute-start | bytes 6291464 | tf_op jit(solution)/shard_map/ppermute | solution.py:12
  257.5 8.7 %collective-permute-start.4 = (f32[16,32768]{1,0:T(8,128)S(1)}, f32[16,32768]{1,0:T(8,128)}, u32[]{:S(2)}, u32[]{:S(2)}) collective-permute-start(f32[16,32768]{1,0:T(8,128)S(1)} %multiply_add_fusion.3), channel_id=1, source_target_pairs={{0,1},{1,0},{2,3},{3,2},{4,5},{5,4},{6,7},{7,6},{8,9},{9,8},{10,11... | collective-permute-start | bytes 6291464 | tf_op jit(solution)/shard_map/ppermute | solution.py:12
  269.3 47.2 %collective-permute-start.5 = (f32[16,32768]{1,0:T(8,128)}, f32[16,32768]{1,0:T(8,128)}, u32[]{:S(2)}, u32[]{:S(2)}) collective-permute-start(f32[16,32768]{1,0:T(8,128)} %multiply_add_fusion.2), channel_id=1, source_target_pairs={{0,2},{1,3},{2,0},{3,1},{4,6},{5,7},{6,4},{7,5},{8,10},{9,11},{10,... | collective-permute-start | bytes 6291464 | tf_op jit(solution)/shard_map/ppermute | solution.py:12
  270.6 51.2 %copy-start.5 = (s32[8192]{0:T(1024)S(1)}, s32[8192]{0:T(1024)}, u32[]{:S(2)}) copy-start(s32[8192]{0:T(1024)} %param.10) | copy-start | bytes 98308
  318.9 47.6 %collective-permute-start.6 = (f32[16,32768]{1,0:T(8,128)S(1)}, f32[16,32768]{1,0:T(8,128)}, u32[]{:S(2)}, u32[]{:S(2)}) collective-permute-start(f32[16,32768]{1,0:T(8,128)S(1)} %multiply_add_fusion.1), channel_id=1, source_target_pairs={{0,4},{1,5},{2,6},{3,7},{4,0},{5,1},{6,2},{7,3},{8,12},{9,13},{10,... | collective-permute-start | bytes 6291464 | tf_op jit(solution)/shard_map/ppermute | solution.py:12
  379.4 33.5 %copy-start.6 = (s32[16]{0:T(128)S(1)}, s32[16]{0:T(128)}, u32[]{:S(2)}) copy-start(s32[16]{0:T(128)} %param.11) | copy-start | bytes 196
  412.9 6.3 %copy-start.7 = (u32[128]{0:T(128)S(1)}, u32[128]{0:T(128)}, u32[]{:S(2)}) copy-start(u32[128]{0:T(128)} %constant.92) | copy-start | bytes 1540
  419.2 128.0 %reduce-scatter.4.cloned.1.call-start = ((), (), s32[]{:S(2)}) async-start(), calls=%async_computation.2 | async-start | bytes 4718592
Sparse Core Ops, SparseCore 0:
  419.3 87.7 all-reduce.2
  511.5 35.5 reduce-scatter.3
where the time goes:
time: 559 us; the launch traced here: 556 us
  waiting for transfers between devices  420 us (75%)
  local copies, waits for them, and re-layouts  59.4 us (11%)
  other arithmetic  27.1 us (5%)
  starting transfers between devices  25.6 us (5%)
  between operations  13.6 us (2%)
  matrix products  10.6 us (2%)
    ppermute x7, waiting for transfers between devices, partner_2(): lax.ppermute(value, axis, [(i, i ^ 1 << bit) for i in range(lax.axis_size...  266 us
    unnamed x4, waiting for transfers between devices  123 us
    gather x1, local copies, waits for them, and re-layouts, per_device(): picked = jnp.take(transformed, sample_local, axis=1)  33.5 us
    all_to_all x1, waiting for transfers between devices, per_device(): lax.all_to_all(gradients, 'ex', split_axis=1, concat_axis=0, tiled=True)  30 us
    add x7, other arithmetic, per_device(): transformed = partner + own_sign * transformed  19.1 us
    ppermute x7, starting transfers between devices, partner_2(): lax.ppermute(value, axis, [(i, i ^ 1 << bit) for i in range(lax.axis_size...  16.6 us
    unnamed x23, local copies, waits for them, and re-layouts  16 us
  transfers between devices with their start and end apart: 10, of which 10 were waited for; matrix products, arithmetic and copies ran while one was open for 0% of the time, Pallas kernels for 0%

commit v1 on v0

v1 whole, which is shorter than its diff:
```python
import functools

import jax
import jax.numpy as jnp
from jax import lax
from jax.experimental import pallas as pl
from jax.experimental.pallas import tpu as pltpu
from jax.sharding import PartitionSpec as P

MESH = pl.DeviceIdType.MESH
BETA_ONE = 0.9
BETA_TWO = 0.999
RING = 4
EX = RING * RING
BF = 2 * RING
DEPTH = 256
ROWS = 16
CHUNK = DEPTH * ROWS
TILE = 1024

STEPS = [(2, 2), (1, 1), (3, 3), (2, 0), (0, 2), (1, 3), (3, 1), (2, 1), (1, 2), (2, 3), (3, 2), (0, 1), (1, 0), (0, 3), (3, 0)]


def parity_sign(values):
    values = values ^ (values >> 4)
    values = values ^ (values >> 2)
    values = values ^ (values >> 1)
    return 1 - 2 * (values & 1)


def kernel(
    g_ref, one_ref, two_ref, flip_ref, rows_ref, pool_ref, out_ref,
    recv, one, two, flip, weight, sign_low, sign_high, high, low, part, got_core, half, got_x, mine, got_ex,
    local_sem, send_sem, recv_sem, core_sem, x_send, x_recv, ex_send, ex_recv,
):
    ex = lax.axis_index("ex")
    bf = lax.axis_index("bf")
    z, y = ex // RING, ex % RING
    x, core = bf // 2, bf % 2
    block_len = g_ref.shape[1]
    count = rows_ref.shape[1]
    chunks = block_len // CHUNK
    width = count // BF

    def owner(dz, dy):
        return (z + dz) % RING * RING + (y + dy) % RING

    def x_peer(dx):
        return (x + dx) % RING * 2 + core

    sibling = x * 2 + 1 - core

    barrier = pltpu.get_barrier_semaphore()
    for dz, dy in STEPS:
        pl.semaphore_signal(barrier, inc=1, device_id=(owner(dz, dy), bf), device_id_type=MESH)
    for dx in (1, 2, 3):
        pl.semaphore_signal(barrier, inc=1, device_id=(ex, x_peer(dx)), device_id_type=MESH)
    pl.semaphore_signal(barrier, inc=1, device_id=(ex, sibling), device_id_type=MESH)

    moments = [
        pltpu.make_async_copy(one_ref, one, local_sem.at[0]),
        pltpu.make_async_copy(two_ref, two, local_sem.at[1]),
        pltpu.make_async_copy(flip_ref, flip, local_sem.at[2]),
    ]
    for copy in moments:
        copy.start()

    pl.semaphore_wait(barrier, EX - 1 + RING)

    def columns(chunk):
        return pl.ds(pl.multiple_of(chunk * CHUNK, CHUNK), CHUNK)

    def send_chunk(chunk, carry):
        for step, (dz, dy) in enumerate(STEPS):
            target = owner(dz, dy)
            pltpu.make_async_remote_copy(
                src_ref=g_ref.at[target, columns(chunk)],
                dst_ref=recv.at[ex, columns(chunk)],
                send_sem=send_sem.at[step],
                recv_sem=recv_sem.at[chunk],
                device_id=(target, bf),
                device_id_type=MESH,
            ).start()
        pltpu.make_async_copy(
            g_ref.at[ex, columns(chunk)], recv.at[ex, columns(chunk)], recv_sem.at[chunk]
        ).start()
        return carry

    lax.fori_loop(0, chunks, send_chunk, 0)

    device = ex * BF + bf
    for b in range(BF):
        source = b % RING * 2 + b // RING
        rows = rows_ref[:, source * width : (source + 1) * width]
        place = slice(b * width, (b + 1) * width)
        lanes = rows & (DEPTH - 1)
        index = lax.broadcasted_iota(jnp.int32, (16, width), 0)
        fine = parity_sign((lanes & 15) & index).astype(jnp.float32).astype(jnp.bfloat16)
        coarse = parity_sign((lanes >> 4) & index).astype(jnp.float32).astype(jnp.bfloat16)
        for i in range(16):
            weight[i * 16 : (i + 1) * 16, place] = fine * coarse[i : i + 1, :]
        sign_low[:, place] = parity_sign(((rows >> 8) & (ROWS - 1)) & index).astype(jnp.float32)
        index = lax.broadcasted_iota(jnp.int32, (chunks, width), 0)
        own = parity_sign((rows >> 15) & device)
        sign_high[:, place] = (own * parity_sign((rows >> 12) & (chunks - 1) & index)).astype(jnp.float32)
    part[...] = jnp.zeros_like(part)

    for copy in moments:
        copy.wait()

    def do_chunk(chunk, carry):
        pltpu.make_async_copy(recv.at[:, columns(chunk)], recv.at[:, columns(chunk)], recv_sem.at[chunk]).wait()
        for j in range(ROWS):
            span = pl.ds(pl.multiple_of(chunk * CHUNK + j * DEPTH, DEPTH), DEPTH)
            grad = recv[:, span]
            moment_new = BETA_ONE * one[:, span] + (1.0 - BETA_ONE) * grad
            second_new = BETA_TWO * two[:, span] + (1.0 - BETA_TWO) * grad * grad
            feature = flip[:, span].astype(jnp.float32) * moment_new * lax.rsqrt(second_new)
            top = feature.astype(jnp.bfloat16)
            high[j * 16 : (j + 1) * 16, :] = top
            low[j * 16 : (j + 1) * 16, :] = (feature - top.astype(jnp.float32)).astype(jnp.bfloat16)

        def tile(t, inner):
            place = pl.ds(pl.multiple_of(t * TILE, TILE), TILE)
            w = weight[:, place]
            product = jnp.dot(high[...], w, preferred_element_type=jnp.float32)
            product = product + jnp.dot(low[...], w, preferred_element_type=jnp.float32)
            sign = sign_low[:, place]
            total = product[0:16] * sign[0:1]
            for j in range(1, ROWS):
                total = total + product[j * 16 : (j + 1) * 16] * sign[j : j + 1]
            part[:, place] = part[:, place] + total * sign_high[pl.ds(chunk, 1), place]
            return inner

        return lax.fori_loop(0, count // TILE, tile, carry, unroll=4)

    lax.fori_loop(0, chunks, do_chunk, 0)

    span = count // 2
    to_core = pltpu.make_async_remote_copy(
        src_ref=part.at[:, pl.ds(pl.multiple_of((1 - core) * span, span), span)],
        dst_ref=got_core,
        send_sem=core_sem.at[0],
        recv_sem=core_sem.at[1],
        device_id=(ex, sibling),
        device_id_type=MESH,
    )
    to_core.start()
    to_core.wait()
    half[...] = part[:, pl.ds(pl.multiple_of(core * span, span), span)] + got_core[...]

    to_x = []
    for dx in (1, 2, 3):
        other = (x + dx) % RING
        copy = pltpu.make_async_remote_copy(
            src_ref=half.at[:, pl.ds(pl.multiple_of(other * width, width), width)],
            dst_ref=got_x.at[dx - 1],
            send_sem=x_send.at[dx - 1],
            recv_sem=x_recv.at[dx - 1],
            device_id=(ex, x_peer(dx)),
            device_id_type=MESH,
        )
        copy.start()
        to_x.append(copy)
    for copy in to_x:
        copy.wait()
    summed = half[:, pl.ds(pl.multiple_of(x * width, width), width)] + got_x[0] + got_x[1] + got_x[2]

    row = lax.broadcasted_iota(jnp.int32, (EX, width), 0)
    pooled = jnp.zeros((EX, width), jnp.float32)
    for e in range(EX):
        pooled = pooled + jnp.where(row == pool_ref[e], summed[e : e + 1], 0.0)
    mine[...] = pooled
    to_ex = []
    for step, (dz, dy) in enumerate(STEPS):
        target = owner(dz, dy)
        copy = pltpu.make_async_remote_copy(
            src_ref=mine.at[target],
            dst_ref=got_ex.at[ex],
            send_sem=ex_send,
            recv_sem=ex_recv,
            device_id=(target, bf),
            device_id_type=MESH,
        )
        copy.start()
    pltpu.make_async_copy(mine.at[ex], got_ex.at[ex], ex_recv).start()
    pltpu.make_async_copy(got_ex, got_ex, ex_recv).wait()
    scale = float(block_len * EX * BF) ** -0.5
    out_ref[...] = jnp.sum(got_ex[...], axis=0, keepdims=True) * scale
    for step in range(len(STEPS)):
        pltpu.make_async_copy(mine.at[0], mine.at[0], ex_send).wait()
        pltpu.make_async_copy(g_ref.at[0], g_ref.at[0], send_sem.at[step]).wait()


def per_device(gradients, moment_one, moment_two, rademacher, sample_rows, pool_order):
    block_len = moment_one.shape[0]
    count = sample_rows.shape[0]
    chunks = block_len // CHUNK
    width = count // BF
    dma = pltpu.SemaphoreType.DMA
    return pl.pallas_call(
        kernel,
        out_shape=jax.ShapeDtypeStruct((1, width), jnp.float32),
        in_specs=[pl.BlockSpec(memory_space=pl.ANY)] * 4
        + [pl.BlockSpec(memory_space=pltpu.VMEM), pl.BlockSpec(memory_space=pltpu.SMEM)],
        out_specs=pl.BlockSpec(memory_space=pltpu.VMEM),
        scratch_shapes=[
            pltpu.VMEM((EX, block_len), jnp.float32),
            pltpu.VMEM((1, block_len), jnp.float32),
            pltpu.VMEM((1, block_len), jnp.float32),
            pltpu.VMEM((1, block_len), jnp.int32),
            pltpu.VMEM((DEPTH, count), jnp.bfloat16),
            pltpu.VMEM((ROWS, count), jnp.float32),
            pltpu.VMEM((chunks, count), jnp.float32),
            pltpu.VMEM((ROWS * EX, DEPTH), jnp.bfloat16),
            pltpu.VMEM((ROWS * EX, DEPTH), jnp.bfloat16),
            pltpu.VMEM((EX, count), jnp.float32),
            pltpu.VMEM((EX, count // 2), jnp.float32),
            pltpu.VMEM((EX, count // 2), jnp.float32),
            pltpu.VMEM((RING - 1, EX, width), jnp.float32),
            pltpu.VMEM((EX, width), jnp.float32),
            pltpu.VMEM((EX, width), jnp.float32),
            dma((3,)),
            dma((len(STEPS),)),
            dma((chunks,)),
            dma((2,)),
            dma((RING - 1,)),
            dma((RING - 1,)),
            dma,
            dma,
        ],
        compiler_params=pltpu.CompilerParams(
            collective_id=0, has_side_effects=True, vmem_limit_bytes=56 * 2**20
        ),
    )(
        gradients.reshape(EX, block_len),
        moment_one.reshape(1, block_len),
        moment_two.reshape(1, block_len),
        rademacher.reshape(1, block_len),
        sample_rows.reshape(1, count),
        pool_order,
    )


def solution(mesh):
    in_specs = (P("ex", None, "bf"), P(("ex", "bf")), P(("ex", "bf")), P(("ex", "bf")), P(), P())
    out_specs = P("ex", "bf")
    return jax.shard_map(
        per_device, mesh=mesh, in_specs=in_specs, out_specs=out_specs, check_vma=False
    )
```

time: 559 us -> 52.5 us (0.09)
  waiting for transfers between devices: 420 us -> 0 us
  local copies, waits for them, and re-layouts: 59.4 us -> 1.28 us
  Pallas kernels: 0 us -> 51 us
  other arithmetic: 27.1 us -> 0 us
  starting transfers between devices: 25.6 us -> 0 us
  between operations: 13.6 us -> 0.01 us
  matrix products: 10.6 us -> 0 us
    ppermute x7 -> x0, waiting for transfers between devices: 266 us -> none  [partner_2(): lax.ppermute(value, axis, [(i, i ^ 1 << bit) for i in range(lax.axis_size...]
    unnamed x4 -> x0, waiting for transfers between devices: 123 us -> none
    pallas_call x0 -> x1, Pallas kernels: none -> 51 us  [per_device(): pl.pallas_call(kernel, out_shape=jax.ShapeDtypeStruct((1, width), jnp.flo...]
    gather x1 -> x0, local copies, waits for them, and re-layouts: 33.5 us -> none  [per_device(): picked = jnp.take(transformed, sample_local, axis=1)]
    all_to_all x1 -> x0, waiting for transfers between devices: 30 us -> none  [per_device(): lax.all_to_all(gradients, 'ex', split_axis=1, concat_axis=0, tiled=True)]
    add x7 -> x0, other arithmetic: 19.1 us -> none  [per_device(): transformed = partner + own_sign * transformed]
    ppermute x7 -> x0, starting transfers between devices: 16.6 us -> none  [partner_2(): lax.ppermute(value, axis, [(i, i ^ 1 << bit) for i in range(lax.axis_size...]
    unnamed x23 -> x1, local copies, waits for them, and re-layouts: 16 us -> 1.28 us
  transfers between devices with their start and end apart: 10 -> 0, of which waited for: 10 -> 0; matrix products, arithmetic and copies ran while one was open for 0% -> 0% of each run, Pallas kernels for 0% -> 0%
where the time goes in v1:
time: 52.5 us; the launch traced here: 52.3 us
  Pallas kernels  51 us (97%)
  local copies, waits for them, and re-layouts  1.28 us (2%)
    pallas_call x1, Pallas kernels, per_device(): pl.pallas_call(kernel, out_shape=jax.ShapeDtypeStruct((1, width), jnp.flo...  51 us
    unnamed x1, local copies, waits for them, and re-layouts  1.28 us

profile of v1, /device:TPU:1, one launch (start us, length us, event | category | flops | bytes accessed | tf_op | source)
XLA Modules:
  0.0 52.3 jit_solution(176982470762668385)
XLA Ops:
  0.0 51.0 %shard_map.64 = f32[1,1024]{1,0:T(1,128)} custom-call(f32[16,32768]{1,0:T(8,128)} %bitcast.5, f32[1,32768]{1,0:T(1,128)} %bitcast.6, f32[1,32768]{1,0:T(1,128)} %bitcast.7, s32[1,32768]{1,0:T(1,128)} %bitcast.8, s32[1,8192]{1,0:T(1,128)} %bitcast.9, s32[16]{0:T(128)} %pool_ref.1), custom_call_target="tpu_custom_call" | custom-call | tf_op jit(solution)/shard_map/pallas_call | solution.py:201
  51.0 1.3 %copy.8 = f32[1,1024]{1,0:T(1,128)} copy(f32[1,1024]{1,0:T(1,128)} %shard_map.64) | data formatting | bytes 8192

commit v2 on v1

v2 whole, which is shorter than its diff:
```python
import functools

import jax
import jax.numpy as jnp
from jax import lax
from jax.experimental import pallas as pl
from jax.experimental.pallas import tpu as pltpu
from jax.sharding import PartitionSpec as P

MESH = pl.DeviceIdType.MESH
BETA_ONE = 0.9
BETA_TWO = 0.999
RING = 4
EX = RING * RING
BF = 2 * RING
DEPTH = 256
ROWS = 16
CHUNK = DEPTH * ROWS

STEPS = [(2, 2), (1, 1), (3, 3), (2, 0), (0, 2), (1, 3), (3, 1), (2, 1), (1, 2), (2, 3), (3, 2), (0, 1), (1, 0), (0, 3), (3, 0)]


def parity_sign(values):
    values = values ^ (values >> 4)
    values = values ^ (values >> 2)
    values = values ^ (values >> 1)
    return 1 - 2 * (values & 1)


def kernel(
    g_ref, one_ref, two_ref, flip_ref, rows_ref, pool_ref, out_ref,
    recv, one, two, flip, weight, sign_low, sign_high, sign_row, high, low, part, outbox, inbox, mine, got_ex,
    g_send, g_recv, m_send, m_recv, bf_send, bf_recv, ex_send, ex_recv,
):
    ex = lax.axis_index("ex")
    bf = lax.axis_index("bf")
    z, y = ex // RING, ex % RING
    block_len = g_ref.shape[1]
    count = rows_ref.shape[1]
    side_len = block_len // 2
    chunks = side_len // CHUNK
    width = count // BF

    def owner(dz, dy):
        return (z + dz) % RING * RING + (y + dy) % RING

    barrier = pltpu.get_barrier_semaphore()
    for dz, dy in STEPS:
        pl.semaphore_signal(barrier, inc=1, device_id=(owner(dz, dy), bf), device_id_type=MESH)
    for d in range(1, BF):
        pl.semaphore_signal(barrier, inc=1, device_id=(ex, (bf + d) % BF), device_id_type=MESH)
    pl.semaphore_wait(barrier, EX - 1 + BF - 1)

    moments = ((one_ref, one), (two_ref, two), (flip_ref, flip))

    def send_chunk(chunk, carry):
        for side in (0, 1):
            own, other = (y, z) if side == 0 else (z, y)
            source = pl.ds(pl.multiple_of(side * side_len + chunk * CHUNK, CHUNK), CHUNK)
            place = pl.ds(pl.multiple_of(chunk * CHUNK, CHUNK), CHUNK)
            step = side * chunks + chunk
            for d in (2, 1, 3):
                along = (own + d) % RING
                target = z * RING + along if side == 0 else along * RING + y
                for i in range(RING):
                    row = i * RING + along if side == 0 else along * RING + i
                    pltpu.make_async_remote_copy(
                        src_ref=g_ref.at[row, source],
                        dst_ref=recv.at[side, i * RING + own, place],
                        send_sem=g_send,
                        recv_sem=g_recv.at[step],
                        device_id=(target, bf),
                        device_id_type=MESH,
                    ).start()
            for d in (2, 1, 3):
                along = (other + d) % RING
                target = along * RING + y if side == 0 else z * RING + along
                for k, (src, dst) in enumerate(moments):
                    pltpu.make_async_remote_copy(
                        src_ref=src.at[0, source],
                        dst_ref=dst.at[side, other, place],
                        send_sem=m_send.at[k],
                        recv_sem=m_recv.at[k, step],
                        device_id=(target, bf),
                        device_id_type=MESH,
                    ).start()
            for i in range(RING):
                row = i * RING + own if side == 0 else own * RING + i
                pltpu.make_async_copy(
                    g_ref.at[row, source], recv.at[side, i * RING + own, place], g_recv.at[step]
                ).start()
            for k, (src, dst) in enumerate(moments):
                pltpu.make_async_copy(src.at[0, source], dst.at[side, other, place], m_recv.at[k, step]).start()
        return carry

    lax.fori_loop(0, chunks, send_chunk, 0)

    for b in range(BF):
        place = slice(b * width, (b + 1) * width)
        rows = rows_ref[:, place]
        lanes = rows & (DEPTH - 1)
        block = rows >> 15
        index = lax.broadcasted_iota(jnp.int32, (16, width), 0)
        fine = parity_sign((lanes & 15) & index).astype(jnp.float32).astype(jnp.bfloat16)
        coarse = parity_sign((lanes >> 4) & index).astype(jnp.float32).astype(jnp.bfloat16)
        for i in range(16):
            weight[i * 16 : (i + 1) * 16, place] = fine * coarse[i : i + 1, :]
        sign_low[:, place] = parity_sign(((rows >> 8) & (ROWS - 1)) & index).astype(jnp.float32)
        index = lax.broadcasted_iota(jnp.int32, (chunks, width), 0)
        index_row = lax.broadcasted_iota(jnp.int32, (RING, width), 0)
        for side in (0, 1):
            own = parity_sign(block & (y * BF + bf if side == 0 else z * RING * BF + bf))
            step_sign = parity_sign((rows >> 12) & (side * chunks + index))
            sign_high[side, :, place] = (own * step_sign).astype(jnp.float32)
            other = (block >> 5 if side == 0 else block >> 3) & (RING - 1)
            sign_row[side, :, place] = parity_sign(other & index_row).astype(jnp.float32)
    part[...] = jnp.zeros_like(part)

    first = lax.broadcasted_iota(jnp.int32, (8, DEPTH), 0) < RING

    def features(side, chunk):
        step = side * chunks + chunk
        place = pl.ds(pl.multiple_of(chunk * CHUNK, CHUNK), CHUNK)
        whole = recv.at[side, :, place]
        pltpu.make_async_copy(whole, whole, g_recv.at[step]).wait()
        for k, (_, dst) in enumerate(moments):
            whole = dst.at[side, :, place]
            pltpu.make_async_copy(whole, whole, m_recv.at[k, step]).wait()
        for j in range(ROWS):
            span = pl.ds(pl.multiple_of(chunk * CHUNK + j * DEPTH, DEPTH), DEPTH)
            found = []
            for h in (0, 1):
                grad = recv[side, 8 * h : 8 * h + 8, span]

                def both(ref):
                    return jnp.where(first, ref[side, 2 * h : 2 * h + 1, span], ref[side, 2 * h + 1 : 2 * h + 2, span])

                moment_new = BETA_ONE * both(one) + (1.0 - BETA_ONE) * grad
                second_new = BETA_TWO * both(two) + (1.0 - BETA_TWO) * grad * grad
                found.append(both(flip).astype(jnp.float32) * moment_new * lax.rsqrt(second_new))
            feature = jnp.concatenate(found, axis=0)
            top = feature.astype(jnp.bfloat16)
            high[j * 16 : (j + 1) * 16, :] = top
            low[j * 16 : (j + 1) * 16, :] = (feature - top.astype(jnp.float32)).astype(jnp.bfloat16)

    def tile(side, chunk, t):
        place = pl.ds(pl.multiple_of(t * width, width), width)
        w = weight[:, place]
        product = jnp.dot(high[...], w, preferred_element_type=jnp.float32)
        product = product + jnp.dot(low[...], w, preferred_element_type=jnp.float32)
        sign = sign_low[:, place]
        total = product[0:16] * sign[0:1]
        for j in range(1, ROWS):
            total = total + product[j * 16 : (j + 1) * 16] * sign[j : j + 1]
        return part[side, :, place] + total * sign_high[side, pl.ds(chunk, 1), place]

    def step_chunk(step, carry):
        side, chunk = step % 2, step // 2
        features(side, chunk)
        for t in range(BF):
            part[side, :, t * width : (t + 1) * width] = tile(side, chunk, t)
        return carry

    lax.fori_loop(0, 2 * chunks - 1, step_chunk, 0)

    def by_example(side, total, place):
        sign = sign_row[side, :, place]
        found = total[0:RING] * sign[0:1]
        for i in range(1, RING):
            found = found + total[i * RING : (i + 1) * RING] * sign[i : i + 1]
        return found

    features(1, chunks - 1)
    sends = []
    for d in range(1, BF + 1):
        t = (bf + d) % BF
        place = pl.ds(pl.multiple_of(t * width, width), width)
        found = jnp.concatenate(
            [by_example(0, part[0, :, place], place), by_example(1, tile(1, chunks - 1, t), place)], axis=0
        )
        if d == BF:
            inbox[BF - 1] = found
        else:
            outbox[d - 1] = found
            copy = pltpu.make_async_remote_copy(
                src_ref=outbox.at[d - 1],
                dst_ref=inbox.at[d - 1],
                send_sem=bf_send.at[d - 1],
                recv_sem=bf_recv.at[d - 1],
                device_id=(ex, t),
                device_id_type=MESH,
            )
            copy.start()
            sends.append(copy)
    summed = inbox[BF - 1]
    for d, copy in enumerate(sends):
        copy.wait_recv()
        summed = summed + inbox[d]

    row = lax.broadcasted_iota(jnp.int32, (EX, width), 0)
    pooled = jnp.zeros((EX, width), jnp.float32)
    for i in range(RING):
        pooled = pooled + jnp.where(row == pool_ref[z * RING + i], summed[i : i + 1], 0.0)
        pooled = pooled + jnp.where(row == pool_ref[i * RING + y], summed[RING + i : RING + i + 1], 0.0)
    mine[...] = pooled
    for dz, dy in STEPS:
        target = owner(dz, dy)
        pltpu.make_async_remote_copy(
            src_ref=mine.at[target],
            dst_ref=got_ex.at[ex],
            send_sem=ex_send,
            recv_sem=ex_recv,
            device_id=(target, bf),
            device_id_type=MESH,
        ).start()
    pltpu.make_async_copy(mine.at[ex], got_ex.at[ex], ex_recv).start()
    for copy in sends:
        copy.wait_send()
    for part_rows in (8, 4):
        sent = g_ref.at[pl.ds(0, part_rows)]
        pltpu.make_async_copy(sent, sent, g_send).wait()
    for k, (src, _) in enumerate(moments):
        for _ in range(3):
            pltpu.make_async_copy(src, src, m_send.at[k]).wait()
    pltpu.make_async_copy(got_ex, got_ex, ex_recv).wait()
    scale = float(block_len * EX * BF) ** -0.5
    out_ref[...] = jnp.sum(got_ex[...], axis=0, keepdims=True) * scale
    for _ in STEPS:
        pltpu.make_async_copy(mine.at[0], mine.at[0], ex_send).wait()


def per_device(gradients, moment_one, moment_two, rademacher, sample_rows, pool_order):
    block_len = moment_one.shape[0]
    count = sample_rows.shape[0]
    side_len = block_len // 2
    chunks = side_len // CHUNK
    width = count // BF
    dma = pltpu.SemaphoreType.DMA
    return pl.pallas_call(
        kernel,
        out_shape=jax.ShapeDtypeStruct((1, width), jnp.float32),
        in_specs=[pl.BlockSpec(memory_space=pl.ANY)] * 4
        + [pl.BlockSpec(memory_space=pltpu.VMEM), pl.BlockSpec(memory_space=pltpu.SMEM)],
        out_specs=pl.BlockSpec(memory_space=pltpu.VMEM),
        scratch_shapes=[
            pltpu.VMEM((2, EX, side_len), jnp.float32),
            pltpu.VMEM((2, RING, side_len), jnp.float32),
            pltpu.VMEM((2, RING, side_len), jnp.float32),
            pltpu.VMEM((2, RING, side_len), jnp.int32),
            pltpu.VMEM((DEPTH, count), jnp.bfloat16),
            pltpu.VMEM((ROWS, count), jnp.float32),
            pltpu.VMEM((2, chunks, count), jnp.float32),
            pltpu.VMEM((2, RING, count), jnp.float32),
            pltpu.VMEM((ROWS * EX, DEPTH), jnp.bfloat16),
            pltpu.VMEM((ROWS * EX, DEPTH), jnp.bfloat16),
            pltpu.VMEM((2, EX, count), jnp.float32),
            pltpu.VMEM((BF - 1, 2 * RING, width), jnp.float32),
            pltpu.VMEM((BF, 2 * RING, width), jnp.float32),
            pltpu.VMEM((EX, width), jnp.float32),
            pltpu.VMEM((EX, width), jnp.float32),
            dma,
            dma((2 * chunks,)),
            dma((3,)),
            dma((3, 2 * chunks)),
            dma((BF - 1,)),
            dma((BF - 1,)),
            dma,
            dma,
        ],
        compiler_params=pltpu.CompilerParams(
            collective_id=0, has_side_effects=True, vmem_limit_bytes=56 * 2**20
        ),
    )(
        gradients.reshape(EX, block_len),
        moment_one.reshape(1, block_len),
        moment_two.reshape(1, block_len),
        rademacher.reshape(1, block_len),
        sample_rows.reshape(1, count),
        pool_order,
    )


def solution(mesh):
    in_specs = (P("ex", None, "bf"), P(("ex", "bf")), P(("ex", "bf")), P(("ex", "bf")), P(), P())
    out_specs = P("ex", "bf")
    return jax.shard_map(
        per_device, mesh=mesh, in_specs=in_specs, out_specs=out_specs, check_vma=False
    )
```

time: 52.5 us -> 45.3 us (0.86)
  Pallas kernels: 51 us -> 43.8 us
    pallas_call x1, Pallas kernels: 51 us -> 43.8 us  [per_device(): pl.pallas_call(kernel, out_shape=jax.ShapeDtypeStruct((1, width), jnp.flo...]
where the time goes in v2:
time: 45.3 us; the launch traced here: 45.1 us
  Pallas kernels  43.8 us (97%)
  local copies, waits for them, and re-layouts  1.28 us (3%)
    pallas_call x1, Pallas kernels, per_device(): pl.pallas_call(kernel, out_shape=jax.ShapeDtypeStruct((1, width), jnp.flo...  43.8 us
    unnamed x1, local copies, waits for them, and re-layouts  1.28 us

profile of v2, /device:TPU:1, one launch (start us, length us, event | category | flops | bytes accessed | tf_op | source)
XLA Modules:
  0.0 45.1 jit_solution(9643980350777152968)
XLA Ops:
  0.0 43.8 %shard_map.64 = f32[1,1024]{1,0:T(1,128)} custom-call(f32[16,32768]{1,0:T(8,128)} %bitcast.5, f32[1,32768]{1,0:T(1,128)} %bitcast.6, f32[1,32768]{1,0:T(1,128)} %bitcast.7, s32[1,32768]{1,0:T(1,128)} %bitcast.8, s32[1,8192]{1,0:T(1,128)} %bitcast.9, s32[16]{0:T(128)} %pool_ref.1), custom_call_target="tpu_custom_call" | custom-call | tf_op jit(solution)/shard_map/pallas_call | solution.py:239
  43.8 1.3 %copy.8 = f32[1,1024]{1,0:T(1,128)} copy(f32[1,1024]{1,0:T(1,128)} %shard_map.64) | data formatting | bytes 8192

commit v3 on v2

--- a/solution.py
+++ b/solution.py
@@ -20,16 +20,16 @@
 STEPS = [(2, 2), (1, 1), (3, 3), (2, 0), (0, 2), (1, 3), (3, 1), (2, 1), (1, 2), (2, 3), (3, 2), (0, 1), (1, 0), (0, 3), (3, 0)]
 
 
-def parity_sign(values):
-    values = values ^ (values >> 4)
-    values = values ^ (values >> 2)
-    values = values ^ (values >> 1)
-    return 1 - 2 * (values & 1)
+def parity_sign(values, bits):
+    while bits > 1:
+        bits = bits // 2
+        values = values ^ (values >> bits)
+    return (1 - 2 * (values & 1)).astype(jnp.float32)
 
 
 def kernel(
     g_ref, one_ref, two_ref, flip_ref, rows_ref, pool_ref, out_ref,
-    recv, one, two, flip, weight, sign_low, sign_high, sign_row, high, low, part, outbox, inbox, mine, got_ex,
+    recv, one, two, flip, weight, coarse, sign_low, sign_high, sign_row, high, low, part, outbox, inbox, mine, got_ex,
     g_send, g_recv, m_send, m_recv, bf_send, bf_recv, ex_send, ex_recv,
 ):
     ex = lax.axis_index("ex")
@@ -53,7 +53,7 @@
 
     moments = ((one_ref, one), (two_ref, two), (flip_ref, flip))
 
-    def send_chunk(chunk, carry):
+    def send_chunk(chunk):
         for side in (0, 1):
             own, other = (y, z) if side == 0 else (z, y)
             source = pl.ds(pl.multiple_of(side * side_len + chunk * CHUNK, CHUNK), CHUNK)
@@ -91,29 +91,29 @@
                 ).start()
             for k, (src, dst) in enumerate(moments):
                 pltpu.make_async_copy(src.at[0, source], dst.at[side, other, place], m_recv.at[k, step]).start()
+
+    send_chunk(0)
+    send_chunk(1)
+
+    index = lax.broadcasted_iota(jnp.int32, (16, width), 0)
+    member = lax.broadcasted_iota(jnp.int32, (8, width), 0)
+    upper = member >= RING
+    step_mask = jnp.where(upper, (z * RING * BF + bf) * block_len, (y * BF + bf) * block_len) + member * CHUNK
+    row_mask = jnp.where(upper, (member - RING) * BF, member * BF * RING) * block_len
+
+    def signs(b, carry):
+        place = pl.ds(pl.multiple_of(b * width, width), width)
+        rows = jnp.broadcast_to(rows_ref[:, place], (16, width))
+        fine = parity_sign(rows & index, 4)
+        coarse[...] = parity_sign((rows >> 4) & index, 4)
+        for i in range(16):
+            weight[i * 16 : (i + 1) * 16, place] = (fine * coarse[i : i + 1, :]).astype(jnp.bfloat16)
+        sign_low[:, place] = parity_sign((rows >> 8) & index, 4)
+        sign_high[:, place] = parity_sign(rows[:8] & step_mask, 32)
+        sign_row[:, place] = parity_sign((rows[:8] & row_mask) >> 18, 4)
         return carry
 
-    lax.fori_loop(0, chunks, send_chunk, 0)
-
-    for b in range(BF):
-        place = slice(b * width, (b + 1) * width)
-        rows = rows_ref[:, place]
-        lanes = rows & (DEPTH - 1)
-        block = rows >> 15
-        index = lax.broadcasted_iota(jnp.int32, (16, width), 0)
-        fine = parity_sign((lanes & 15) & index).astype(jnp.float32).astype(jnp.bfloat16)
-        coarse = parity_sign((lanes >> 4) & index).astype(jnp.float32).astype(jnp.bfloat16)
-        for i in range(16):
-            weight[i * 16 : (i + 1) * 16, place] = fine * coarse[i : i + 1, :]
-        sign_low[:, place] = parity_sign(((rows >> 8) & (ROWS - 1)) & index).astype(jnp.float32)
-        index = lax.broadcasted_iota(jnp.int32, (chunks, width), 0)
-        index_row = lax.broadcasted_iota(jnp.int32, (RING, width), 0)
-        for side in (0, 1):
-            own = parity_sign(block & (y * BF + bf if side == 0 else z * RING * BF + bf))
-            step_sign = parity_sign((rows >> 12) & (side * chunks + index))
-            sign_high[side, :, place] = (own * step_sign).astype(jnp.float32)
-            other = (block >> 5 if side == 0 else block >> 3) & (RING - 1)
-            sign_row[side, :, place] = parity_sign(other & index_row).astype(jnp.float32)
+    lax.fori_loop(0, BF, signs, 0)
     part[...] = jnp.zeros_like(part)
 
     first = lax.broadcasted_iota(jnp.int32, (8, DEPTH), 0) < RING
@@ -152,19 +152,24 @@
         total = product[0:16] * sign[0:1]
         for j in range(1, ROWS):
             total = total + product[j * 16 : (j + 1) * 16] * sign[j : j + 1]
-        return part[side, :, place] + total * sign_high[side, pl.ds(chunk, 1), place]
+        return part[side, :, place] + total * sign_high[pl.ds(side * chunks + chunk, 1), place]
 
     def step_chunk(step, carry):
         side, chunk = step % 2, step // 2
         features(side, chunk)
         for t in range(BF):
             part[side, :, t * width : (t + 1) * width] = tile(side, chunk, t)
+
+        @pl.when((side == 0) & (chunk + 2 < chunks))
+        def _():
+            send_chunk(chunk + 2)
+
         return carry
 
     lax.fori_loop(0, 2 * chunks - 1, step_chunk, 0)
 
     def by_example(side, total, place):
-        sign = sign_row[side, :, place]
+        sign = sign_row[side * RING : (side + 1) * RING, place]
         found = total[0:RING] * sign[0:1]
         for i in range(1, RING):
             found = found + total[i * RING : (i + 1) * RING] * sign[i : i + 1]
@@ -248,9 +253,10 @@
             pltpu.VMEM((2, RING, side_len), jnp.float32),
             pltpu.VMEM((2, RING, side_len), jnp.int32),
             pltpu.VMEM((DEPTH, count), jnp.bfloat16),
+            pltpu.VMEM((16, width), jnp.float32),
             pltpu.VMEM((ROWS, count), jnp.float32),
-            pltpu.VMEM((2, chunks, count), jnp.float32),
-            pltpu.VMEM((2, RING, count), jnp.float32),
+            pltpu.VMEM((2 * chunks, count), jnp.float32),
+            pltpu.VMEM((2 * RING, count), jnp.float32),
             pltpu.VMEM((ROWS * EX, DEPTH), jnp.bfloat16),
             pltpu.VMEM((ROWS * EX, DEPTH), jnp.bfloat16),
             pltpu.VMEM((2, EX, count), jnp.float32),

time: 45.3 us -> 45.8 us (1.011)
  Pallas kernels: 43.8 us -> 44.3 us
    pallas_call x1, Pallas kernels: 43.8 us -> 44.3 us  [per_device(): pl.pallas_call(kernel, out_shape=jax.ShapeDtypeStruct((1, width), jnp.flo...]
where the time goes in v3:
time: 45.8 us; the launch traced here: 45.6 us
  Pallas kernels  44.3 us (97%)
  local copies, waits for them, and re-layouts  1.28 us (3%)
    pallas_call x1, Pallas kernels, per_device(): pl.pallas_call(kernel, out_shape=jax.ShapeDtypeStruct((1, width), jnp.flo...  44.3 us
    unnamed x1, local copies, waits for them, and re-layouts  1.28 us

profile of v3, /device:TPU:1, one launch (start us, length us, event | category | flops | bytes accessed | tf_op | source)
XLA Modules:
  0.0 45.6 jit_solution(4716317607055793806)
XLA Ops:
  0.0 44.3 %shard_map.64 = f32[1,1024]{1,0:T(1,128)} custom-call(f32[16,32768]{1,0:T(8,128)} %bitcast.5, f32[1,32768]{1,0:T(1,128)} %bitcast.6, f32[1,32768]{1,0:T(1,128)} %bitcast.7, s32[1,32768]{1,0:T(1,128)} %bitcast.8, s32[1,8192]{1,0:T(1,128)} %bitcast.9, s32[16]{0:T(128)} %pool_ref.1), custom_call_target="tpu_custom_call" | custom-call | tf_op jit(solution)/shard_map/pallas_call | solution.py:244
  44.3 1.3 %copy.8 = f32[1,1024]{1,0:T(1,128)} copy(f32[1,1024]{1,0:T(1,128)} %shard_map.64) | data formatting | bytes 8192

commit v4 on v3

v4 whole, which is shorter than its diff:
```python
import functools

import jax
import jax.numpy as jnp
from jax import lax
from jax.experimental import pallas as pl
from jax.experimental.pallas import tpu as pltpu
from jax.sharding import PartitionSpec as P

MESH = pl.DeviceIdType.MESH
BETA_ONE = 0.9
BETA_TWO = 0.999
RING = 4
EX = RING * RING
BF = 2 * RING
DEPTH = 256
GROUP = 16
PLAN = [(8, 2), (16, 2), (8, 1), (4, 2)]

STEPS = [(2, 2), (2, 1), (2, 3), (1, 2), (3, 2), (1, 1), (1, 3), (3, 1), (3, 3), (2, 0), (0, 2), (0, 1), (1, 0), (0, 3), (3, 0)]
TILES = [(2, 0), (2, 1), (1, 0), (1, 1), (3, 0), (3, 1), (0, 1)]


def parity_sign(values, bits):
    while bits > 1:
        bits = bits // 2
        values = values ^ (values >> bits)
    return (1 - 2 * (values & 1)).astype(jnp.float32)


def chunk_list():
    start = 0
    for spans, many in PLAN:
        for _ in range(many):
            yield spans, start
            start += spans


def kernel(
    g_ref, one_ref, two_ref, flip_ref, rows_ref, pool_ref, out_ref,
    recv, one, two, flip, weight, coarse, sign_low, sign_high, sign_row, left, part, outbox, inbox, mine, got_ex,
    g_send, g_recv, m_send, m_recv, bf_send, bf_recv, ex_send, ex_recv,
):
    ex = lax.axis_index("ex")
    bf = lax.axis_index("bf")
    z, y = ex // RING, ex % RING
    block_len = g_ref.shape[1]
    count = rows_ref.shape[1]
    side_len = block_len // 2
    width = count // BF
    order = list(chunk_list())

    def owner(dz, dy):
        return (z + dz) % RING * RING + (y + dy) % RING

    def bf_peer(dx, flip_core):
        core = bf % 2
        return (bf // 2 + dx) % RING * 2 + (1 - core if flip_core else core)

    barrier = pltpu.get_barrier_semaphore()
    for d in (2, 1, 3):
        pl.semaphore_signal(barrier, inc=1, device_id=(owner(d, 0), bf), device_id_type=MESH)
        pl.semaphore_signal(barrier, inc=1, device_id=(owner(0, d), bf), device_id_type=MESH)
    for dx, flip_core in TILES:
        pl.semaphore_signal(barrier, inc=1, device_id=(ex, bf_peer(dx, flip_core)), device_id_type=MESH)
    pl.semaphore_wait(barrier, 2 * (RING - 1) + BF - 1)

    moments = ((one_ref, one), (two_ref, two), (flip_ref, flip))

    def send_chunk(number, spans, first):
        size = spans * DEPTH
        for side in (0, 1):
            own, other = (y, z) if side == 0 else (z, y)
            source = pl.ds(side * side_len + first * DEPTH, size)
            place = pl.ds(first * DEPTH, size)
            for d in (2, 1, 3):
                along = (own + d) % RING
                target = z * RING + along if side == 0 else along * RING + y
                for i in range(RING):
                    row = i * RING + along if side == 0 else along * RING + i
                    pltpu.make_async_remote_copy(
                        src_ref=g_ref.at[row, source],
                        dst_ref=recv.at[side, i * RING + own, place],
                        send_sem=g_send,
                        recv_sem=g_recv.at[side, number],
                        device_id=(target, bf),
                        device_id_type=MESH,
                    ).start()
            for d in (2, 1, 3):
                along = (other + d) % RING
                target = along * RING + y if side == 0 else z * RING + along
                for k, (src, dst) in enumerate(moments):
                    pltpu.make_async_remote_copy(
                        src_ref=src.at[0, source],
                        dst_ref=dst.at[side, other, place],
                        send_sem=m_send.at[k],
                        recv_sem=m_recv.at[k, side, number],
                        device_id=(target, bf),
                        device_id_type=MESH,
                    ).start()
            for i in range(RING):
                row = i * RING + own if side == 0 else own * RING + i
                pltpu.make_async_copy(
                    g_ref.at[row, source], recv.at[side, i * RING + own, place], g_recv.at[side, number]
                ).start()
            for k, (src, dst) in enumerate(moments):
                pltpu.make_async_copy(
                    src.at[0, source], dst.at[side, other, place], m_recv.at[k, side, number]
                ).start()

    for number, (spans, first) in enumerate(order):
        send_chunk(number, spans, first)

    index = lax.broadcasted_iota(jnp.int32, (16, width), 0)
    member = lax.broadcasted_iota(jnp.int32, (8, width), 0)
    upper = member >= RING
    step_mask = jnp.where(upper, (z * RING * BF + bf) * block_len, (y * BF + bf) * block_len) + member * (GROUP * DEPTH)
    row_mask = jnp.where(upper, (member - RING) * BF, member * BF * RING) * block_len

    def signs(b, carry):
        place = pl.ds(pl.multiple_of(b * width, width), width)
        rows = jnp.broadcast_to(rows_ref[:, place], (16, width))
        fine = parity_sign(rows & index, 4)
        coarse[...] = parity_sign((rows >> 4) & index, 4)
        for i in range(16):
            weight[i * 16 : (i + 1) * 16, place] = (fine * coarse[i : i + 1, :]).astype(jnp.bfloat16)
        sign_low[:, place] = parity_sign((rows >> 8) & index, 4)
        sign_high[:, place] = parity_sign(rows[:8] & step_mask, 32)
        sign_row[:, place] = parity_sign((rows[:8] & row_mask) >> 18, 4)
        return carry

    lax.fori_loop(0, BF, signs, 0)
    part[...] = jnp.zeros_like(part)

    above = lax.broadcasted_iota(jnp.int32, (8, DEPTH), 0) < RING

    def features(side, number, spans, first):
        size = spans * DEPTH
        place = pl.ds(pl.multiple_of(first * DEPTH, 4 * DEPTH), size)
        whole = recv.at[side, :, place]
        pltpu.make_async_copy(whole, whole, g_recv.at[side, number]).wait()
        for k, (_, dst) in enumerate(moments):
            whole = dst.at[side, :, place]
            pltpu.make_async_copy(whole, whole, m_recv.at[k, side, number]).wait()
        for j in range(spans):
            span = pl.ds(pl.multiple_of((first + j) * DEPTH, DEPTH), DEPTH)
            found = []
            for h in (0, 1):
                grad = recv[side, 8 * h : 8 * h + 8, span]

                def both(ref):
                    return jnp.where(above, ref[side, 2 * h : 2 * h + 1, span], ref[side, 2 * h + 1 : 2 * h + 2, span])

                moment_new = BETA_ONE * both(one) + (1.0 - BETA_ONE) * grad
                second_new = BETA_TWO * both(two) + (1.0 - BETA_TWO) * grad * grad
                found.append(both(flip).astype(jnp.float32) * moment_new * lax.rsqrt(second_new))
            feature = jnp.concatenate(found, axis=0)
            top = feature.astype(jnp.bfloat16)
            left[j * 16 : (j + 1) * 16, :] = top
            rest = (feature - top.astype(jnp.float32)).astype(jnp.bfloat16)
            left[(spans + j) * 16 : (spans + j + 1) * 16, :] = rest

    def tile(side, spans, first, t):
        place = pl.ds(pl.multiple_of(t * width, width), width)
        w = weight[:, place]
        product = jnp.dot(left[: 2 * spans * 16], w, preferred_element_type=jnp.float32)
        product = product[: spans * 16] + product[spans * 16 :]
        sign = sign_low[pl.ds(pl.multiple_of(first % GROUP // 8 * 8, 8), max(spans, 8)), place]
        if spans == 4:
            sign = jnp.where(first % 8 == 4, sign[4:8], sign[0:4])
        total = product[0:16] * sign[0:1]
        for j in range(1, spans):
            total = total + product[j * 16 : (j + 1) * 16] * sign[j : j + 1]
        step_sign = sign_high[pl.ds(side * (side_len // (GROUP * DEPTH)) + first // GROUP, 1), place]
        return part[side, :, place] + total * step_sign

    def do_chunk(side, number, spans, first):
        features(side, number, spans, first)
        for t in range(BF):
            part[side, :, t * width : (t + 1) * width] = tile(side, spans, first, t)

    def by_example(side, total, place):
        sign = sign_row[side * RING : (side + 1) * RING, place]
        found = total[0:RING] * sign[0:1]
        for i in range(1, RING):
            found = found + total[i * RING : (i + 1) * RING] * sign[i : i + 1]
        return found

    def bf_copy(side, slot):
        return pltpu.make_async_remote_copy(
            src_ref=outbox.at[side, slot],
            dst_ref=inbox.at[side, slot],
            send_sem=bf_send.at[side, slot],
            recv_sem=bf_recv.at[side, slot],
            device_id=(ex, bf_peer(*TILES[slot])),
            device_id_type=MESH,
        )

    number, start = 0, 0
    for spans, many in PLAN:

        def step_chunk(step, carry, spans=spans, number=number, start=start):
            do_chunk(step % 2, number + step // 2, spans, start + step // 2 * spans)
            return carry

        steps = 2 * many - (2 if number + many == len(order) else 0)
        lax.fori_loop(0, steps, step_chunk, 0)
        number, start = number + many, start + many * spans

    number, (spans, first) = len(order) - 1, order[-1]
    tiles = [bf_peer(*peer) for peer in TILES] + [bf]
    do_chunk(0, number, spans, first)
    for side in (0, 1):
        if side == 1:
            features(side, number, spans, first)
        for slot, t in enumerate(tiles):
            place = pl.ds(pl.multiple_of(t * width, width), width)
            total = part[side, :, place] if side == 0 else tile(side, spans, first, t)
            if slot < len(TILES):
                outbox[side, slot] = by_example(side, total, place)
                bf_copy(side, slot).start()
            else:
                inbox[side, slot] = by_example(side, total, place)
    summed = []
    for side in (0, 1):
        found = inbox[side, BF - 1]
        for slot in range(BF - 1):
            bf_copy(side, slot).wait_recv()
            found = found + inbox[side, slot]
        summed.append(found)

    row = lax.broadcasted_iota(jnp.int32, (EX, width), 0)
    pooled = jnp.zeros((EX, width), jnp.float32)
    for i in range(RING):
        pooled = pooled + jnp.where(row == pool_ref[z * RING + i], summed[0][i : i + 1], 0.0)
        pooled = pooled + jnp.where(row == pool_ref[i * RING + y], summed[1][i : i + 1], 0.0)
    mine[...] = pooled
    for dz, dy in STEPS:
        target = owner(dz, dy)
        pltpu.make_async_remote_copy(
            src_ref=mine.at[target],
            dst_ref=got_ex.at[ex],
            send_sem=ex_send,
            recv_sem=ex_recv,
            device_id=(target, bf),
            device_id_type=MESH,
        ).start()
    pltpu.make_async_copy(mine.at[ex], got_ex.at[ex], ex_recv).start()
    for side in (0, 1):
        for slot in range(BF - 1):
            bf_copy(side, slot).wait_send()
    for part_rows in (8, 4):
        sent = g_ref.at[pl.ds(0, part_rows)]
        pltpu.make_async_copy(sent, sent, g_send).wait()
    for k, (src, _) in enumerate(moments):
        for _ in range(3):
            pltpu.make_async_copy(src, src, m_send.at[k]).wait()
    pltpu.make_async_copy(got_ex, got_ex, ex_recv).wait()
    scale = float(block_len * EX * BF) ** -0.5
    out_ref[...] = jnp.sum(got_ex[...], axis=0, keepdims=True) * scale
    for _ in STEPS:
        pltpu.make_async_copy(mine.at[0], mine.at[0], ex_send).wait()


def per_device(gradients, moment_one, moment_two, rademacher, sample_rows, pool_order):
    block_len = moment_one.shape[0]
    count = sample_rows.shape[0]
    side_len = block_len // 2
    width = count // BF
    chunks = len(list(chunk_list()))
    dma = pltpu.SemaphoreType.DMA
    return pl.pallas_call(
        kernel,
        out_shape=jax.ShapeDtypeStruct((1, width), jnp.float32),
        in_specs=[pl.BlockSpec(memory_space=pl.ANY)] * 4
        + [pl.BlockSpec(memory_space=pltpu.VMEM), pl.BlockSpec(memory_space=pltpu.SMEM)],
        out_specs=pl.BlockSpec(memory_space=pltpu.VMEM),
        scratch_shapes=[
            pltpu.VMEM((2, EX, side_len), jnp.float32),
            pltpu.VMEM((2, RING, side_len), jnp.float32),
            pltpu.VMEM((2, RING, side_len), jnp.float32),
            pltpu.VMEM((2, RING, side_len), jnp.int32),
            pltpu.VMEM((DEPTH, count), jnp.bfloat16),
            pltpu.VMEM((16, width), jnp.float32),
            pltpu.VMEM((GROUP, count), jnp.float32),
            pltpu.VMEM((block_len // (GROUP * DEPTH), count), jnp.float32),
            pltpu.VMEM((2 * RING, count), jnp.float32),
            pltpu.VMEM((2 * GROUP * EX, DEPTH), jnp.bfloat16),
            pltpu.VMEM((2, EX, count), jnp.float32),
            pltpu.VMEM((2, BF - 1, RING, width), jnp.float32),
            pltpu.VMEM((2, BF, RING, width), jnp.float32),
            pltpu.VMEM((EX, width), jnp.float32),
            pltpu.VMEM((EX, width), jnp.float32),
            dma,
            dma((2, chunks)),
            dma((3,)),
            dma((3, 2, chunks)),
            dma((2, BF - 1)),
            dma((2, BF - 1)),
            dma,
            dma,
        ],
        compiler_params=pltpu.CompilerParams(
            collective_id=0, has_side_effects=True, vmem_limit_bytes=56 * 2**20
        ),
    )(
        gradients.reshape(EX, block_len),
        moment_one.reshape(1, block_len),
        moment_two.reshape(1, block_len),
        rademacher.reshape(1, block_len),
        sample_rows.reshape(1, count),
        pool_order,
    )


def solution(mesh):
    in_specs = (P("ex", None, "bf"), P(("ex", "bf")), P(("ex", "bf")), P(("ex", "bf")), P(), P())
    out_specs = P("ex", "bf")
    return jax.shard_map(
        per_device, mesh=mesh, in_specs=in_specs, out_specs=out_specs, check_vma=False
    )
```

time: 45.8 us -> 45.7 us (level)
  no operation moved by 1% of the time
where the time goes in v4:
time: 45.7 us; the launch traced here: 45.5 us
  Pallas kernels  44.2 us (97%)
  local copies, waits for them, and re-layouts  1.28 us (3%)
    pallas_call x1, Pallas kernels, per_device(): pl.pallas_call(kernel, out_shape=jax.ShapeDtypeStruct((1, width), jnp.flo...  44.2 us
    unnamed x1, local copies, waits for them, and re-layouts  1.28 us

profile of v4, /device:TPU:1, one launch (start us, length us, event | category | flops | bytes accessed | tf_op | source)
XLA Modules:
  0.0 45.5 jit_solution(1651781847359215872)
XLA Ops:
  0.0 44.2 %shard_map.64 = f32[1,1024]{1,0:T(1,128)} custom-call(f32[16,32768]{1,0:T(8,128)} %bitcast.5, f32[1,32768]{1,0:T(1,128)} %bitcast.6, f32[1,32768]{1,0:T(1,128)} %bitcast.7, s32[1,32768]{1,0:T(1,128)} %bitcast.8, s32[1,8192]{1,0:T(1,128)} %bitcast.9, s32[16]{0:T(128)} %pool_ref.1), custom_call_target="tpu_custom_call" | custom-call | tf_op jit(solution)/shard_map/pallas_call | solution.py:272
  44.2 1.3 %copy.8 = f32[1,1024]{1,0:T(1,128)} copy(f32[1,1024]{1,0:T(1,128)} %shard_map.64) | data formatting | bytes 8192

commit v5 on v4

--- a/solution.py
+++ b/solution.py
@@ -15,7 +15,9 @@
 BF = 2 * RING
 DEPTH = 256
 GROUP = 16
-PLAN = [(8, 2), (16, 2), (8, 1), (4, 2)]
+PLAN = [(8, 2), (16, 2), (8, 2)]
+LANES = 128
+TILE = 256
 
 STEPS = [(2, 2), (2, 1), (2, 3), (1, 2), (3, 2), (1, 1), (1, 3), (3, 1), (3, 3), (2, 0), (0, 2), (0, 1), (1, 0), (0, 3), (3, 0)]
 TILES = [(2, 0), (2, 1), (1, 0), (1, 1), (3, 0), (3, 1), (0, 1)]
@@ -38,7 +40,7 @@
 
 def kernel(
     g_ref, one_ref, two_ref, flip_ref, rows_ref, pool_ref, out_ref,
-    recv, one, two, flip, weight, coarse, sign_low, sign_high, sign_row, left, part, outbox, inbox, mine, got_ex,
+    recv, one, two, flip, weight, coarse, sign_low, sign_high, sign_row, left, slots, unsort, which, part, outbox, inbox, mine, got_ex,
     g_send, g_recv, m_send, m_recv, bf_send, bf_recv, ex_send, ex_recv,
 ):
     ex = lax.axis_index("ex")
@@ -48,6 +50,7 @@
     count = rows_ref.shape[1]
     side_len = block_len // 2
     width = count // BF
+    slotted = width + TILE
     order = list(chunk_list())
 
     def owner(dz, dy):
@@ -111,25 +114,59 @@
     for number, (spans, first) in enumerate(order):
         send_chunk(number, spans, first)
 
-    index = lax.broadcasted_iota(jnp.int32, (16, width), 0)
-    member = lax.broadcasted_iota(jnp.int32, (8, width), 0)
+    codes = jnp.concatenate([rows_ref[:, b * width : (b + 1) * width] for b in range(BF)], axis=0)
+    bit = (codes >> 8) & 1
+    before = lax.broadcasted_iota(jnp.int32, (LANES, LANES), 0) < lax.broadcasted_iota(jnp.int32, (LANES, LANES), 1)
+    before = jnp.where(before, 1.0, 0.0).astype(jnp.bfloat16)
+    ones = jnp.zeros((BF, 1), jnp.float32)
+    ranks = []
+    for b in range(width // LANES):
+        piece = bit[:, b * LANES : (b + 1) * LANES].astype(jnp.float32)
+        ranks.append(jnp.dot(piece.astype(jnp.bfloat16), before, preferred_element_type=jnp.float32) + ones)
+        ones = ones + jnp.sum(piece, axis=1, keepdims=True)
+    rank = jnp.concatenate(ranks, axis=1).astype(jnp.int32)
+    zeros = width - ones.astype(jnp.int32)
+    lane = lax.broadcasted_iota(jnp.int32, (BF, width), 1)
+    slots[...] = jnp.where(bit == 1, TILE + zeros + rank, lane - rank)
+    for b in range(BF):
+        zero_count = width - jnp.sum(bit[b : b + 1])
+        for u in range(slotted // TILE):
+            which[b * (slotted // TILE) + u] = (u * TILE >= zero_count).astype(jnp.int32)
+
+    def one_hot(slot):
+        index = lax.broadcasted_iota(jnp.int32, (LANES, width), 0)
+        return jnp.where(index == (slot & (LANES - 1)), 1.0, 0.0).astype(jnp.bfloat16)
+
+    index = lax.broadcasted_iota(jnp.int32, (16, slotted), 0)
+    member = lax.broadcasted_iota(jnp.int32, (8, slotted), 0)
     upper = member >= RING
     step_mask = jnp.where(upper, (z * RING * BF + bf) * block_len, (y * BF + bf) * block_len) + member * (GROUP * DEPTH)
     row_mask = jnp.where(upper, (member - RING) * BF, member * BF * RING) * block_len
 
     def signs(b, carry):
-        place = pl.ds(pl.multiple_of(b * width, width), width)
-        rows = jnp.broadcast_to(rows_ref[:, place], (16, width))
+        code = rows_ref[:, pl.ds(pl.multiple_of(b * width, width), width)]
+        slot = slots[pl.ds(b, 1), :]
+        here = lax.broadcasted_iota(jnp.int32, (16, width), 0) == (slot >> 7)
+        pieces = [jnp.where(here, (code >> shift) & 255, 0).astype(jnp.float32) for shift in (0, 8, 16)]
+        pieces = jnp.concatenate(pieces, axis=0).astype(jnp.bfloat16)
+        moved = lax.dot_general(
+            pieces, one_hot(slot), (((1,), (1,)), ((), ())), preferred_element_type=jnp.float32
+        ).astype(jnp.int32)
+        moved = moved[0:16] + (moved[16:32] << 8) + (moved[32:48] << 16)
+        rows = jnp.concatenate([moved[i : i + 1] for i in range(slotted // LANES)], axis=1)
+        rows = jnp.broadcast_to(rows, (16, slotted))
+        place = pl.ds(pl.multiple_of(b * slotted, slotted), slotted)
         fine = parity_sign(rows & index, 4)
         coarse[...] = parity_sign((rows >> 4) & index, 4)
         for i in range(16):
             weight[i * 16 : (i + 1) * 16, place] = (fine * coarse[i : i + 1, :]).astype(jnp.bfloat16)
-        sign_low[:, place] = parity_sign((rows >> 8) & index, 4)
+        sign_low[:, place] = parity_sign((rows[:8] >> 9) & (index[:8] & 7), 4)
         sign_high[:, place] = parity_sign(rows[:8] & step_mask, 32)
         sign_row[:, place] = parity_sign((rows[:8] & row_mask) >> 18, 4)
         return carry
 
-    lax.fori_loop(0, BF, signs, 0)
+    lax.fori_loop(0, BF, signs, 0, unroll=2)
+    unsort[...] = one_hot(slots[pl.ds(bf, 1), :])
     part[...] = jnp.zeros_like(part)
 
     above = lax.broadcasted_iota(jnp.int32, (8, DEPTH), 0) < RING
@@ -142,7 +179,7 @@
         for k, (_, dst) in enumerate(moments):
             whole = dst.at[side, :, place]
             pltpu.make_async_copy(whole, whole, m_recv.at[k, side, number]).wait()
-        for j in range(spans):
+        def feature(j):
             span = pl.ds(pl.multiple_of((first + j) * DEPTH, DEPTH), DEPTH)
             found = []
             for h in (0, 1):
@@ -154,30 +191,40 @@
                 moment_new = BETA_ONE * both(one) + (1.0 - BETA_ONE) * grad
                 second_new = BETA_TWO * both(two) + (1.0 - BETA_TWO) * grad * grad
                 found.append(both(flip).astype(jnp.float32) * moment_new * lax.rsqrt(second_new))
-            feature = jnp.concatenate(found, axis=0)
-            top = feature.astype(jnp.bfloat16)
-            left[j * 16 : (j + 1) * 16, :] = top
-            rest = (feature - top.astype(jnp.float32)).astype(jnp.bfloat16)
-            left[(spans + j) * 16 : (spans + j + 1) * 16, :] = rest
+            return jnp.concatenate(found, axis=0)
+
+        for q in range(spans // 2):
+            even, odd = feature(2 * q), feature(2 * q + 1)
+            for value, combined in ((0, even + odd), (1, even - odd)):
+                top = combined.astype(jnp.bfloat16)
+                rest = (combined - top.astype(jnp.float32)).astype(jnp.bfloat16)
+                left[value, q * 16 : (q + 1) * 16, :] = top
+                at = (spans // 2 + q) * 16
+                left[value, at : at + 16, :] = rest
 
     def tile(side, spans, first, t):
-        place = pl.ds(pl.multiple_of(t * width, width), width)
-        w = weight[:, place]
-        product = jnp.dot(left[: 2 * spans * 16], w, preferred_element_type=jnp.float32)
-        product = product[: spans * 16] + product[spans * 16 :]
-        sign = sign_low[pl.ds(pl.multiple_of(first % GROUP // 8 * 8, 8), max(spans, 8)), place]
-        if spans == 4:
-            sign = jnp.where(first % 8 == 4, sign[4:8], sign[0:4])
-        total = product[0:16] * sign[0:1]
-        for j in range(1, spans):
-            total = total + product[j * 16 : (j + 1) * 16] * sign[j : j + 1]
-        step_sign = sign_high[pl.ds(side * (side_len // (GROUP * DEPTH)) + first // GROUP, 1), place]
-        return part[side, :, place] + total * step_sign
+        half = spans // 2
+        found = []
+        for u in range(slotted // TILE):
+            place = pl.ds(pl.multiple_of(t * slotted + u * TILE, TILE), TILE)
+            value = which[t * (slotted // TILE) + u]
+            rows = left[value, : spans * 16, :]
+            product = jnp.dot(rows, weight[:, place], preferred_element_type=jnp.float32)
+            product = product[: half * 16] + product[half * 16 :]
+            sign = sign_low[:, place]
+            if spans < GROUP:
+                sign = jnp.where(first % GROUP == 8, sign[4:8], sign[0:4])
+            total = product[0:16] * sign[0:1]
+            for j in range(1, half):
+                total = total + product[j * 16 : (j + 1) * 16] * sign[j : j + 1]
+            step_sign = sign_high[pl.ds(side * (side_len // (GROUP * DEPTH)) + first // GROUP, 1), place]
+            found.append(part[side, :, place] + total * step_sign)
+        return jnp.concatenate(found, axis=1)
 
     def do_chunk(side, number, spans, first):
         features(side, number, spans, first)
         for t in range(BF):
-            part[side, :, t * width : (t + 1) * width] = tile(side, spans, first, t)
+            part[side, :, t * slotted : (t + 1) * slotted] = tile(side, spans, first, t)
 
     def by_example(side, total, place):
         sign = sign_row[side * RING : (side + 1) * RING, place]
@@ -214,7 +261,7 @@
         if side == 1:
             features(side, number, spans, first)
         for slot, t in enumerate(tiles):
-            place = pl.ds(pl.multiple_of(t * width, width), width)
+            place = pl.ds(pl.multiple_of(t * slotted, slotted), slotted)
             total = part[side, :, place] if side == 0 else tile(side, spans, first, t)
             if slot < len(TILES):
                 outbox[side, slot] = by_example(side, total, place)
@@ -229,11 +276,26 @@
             found = found + inbox[side, slot]
         summed.append(found)
 
+    found = jnp.concatenate(summed, axis=0)
+    terms = []
+    for _ in range(3):
+        term = found.astype(jnp.bfloat16).astype(jnp.float32)
+        found = found - term
+        terms += [term[:, i * LANES : (i + 1) * LANES] for i in range(slotted // LANES)]
+    stacked = jnp.concatenate(terms, axis=0).astype(jnp.bfloat16)
+    spread = jnp.dot(stacked, unsort[...], preferred_element_type=jnp.float32)
+    size = slotted // LANES * 8
+    spread = spread[:size] + spread[size : 2 * size] + spread[2 * size :]
+    chosen = jnp.broadcast_to(slots[pl.ds(bf, 1), :] >> 7, (8, width))
+    summed = jnp.zeros((8, width), jnp.float32)
+    for i in range(slotted // LANES):
+        summed = summed + jnp.where(chosen == i, spread[8 * i : 8 * i + 8], 0.0)
+
     row = lax.broadcasted_iota(jnp.int32, (EX, width), 0)
     pooled = jnp.zeros((EX, width), jnp.float32)
     for i in range(RING):
-        pooled = pooled + jnp.where(row == pool_ref[z * RING + i], summed[0][i : i + 1], 0.0)
-        pooled = pooled + jnp.where(row == pool_ref[i * RING + y], summed[1][i : i + 1], 0.0)
+        pooled = pooled + jnp.where(row == pool_ref[z * RING + i], summed[i : i + 1], 0.0)
+        pooled = pooled + jnp.where(row == pool_ref[i * RING + y], summed[RING + i : RING + i + 1], 0.0)
     mine[...] = pooled
     for dz, dy in STEPS:
         target = owner(dz, dy)
@@ -267,6 +329,8 @@
     count = sample_rows.shape[0]
     side_len = block_len // 2
     width = count // BF
+    slotted = width + TILE
+    slot_count = slotted * BF
     chunks = len(list(chunk_list()))
     dma = pltpu.SemaphoreType.DMA
     return pl.pallas_call(
@@ -280,15 +344,18 @@
             pltpu.VMEM((2, RING, side_len), jnp.float32),
             pltpu.VMEM((2, RING, side_len), jnp.float32),
             pltpu.VMEM((2, RING, side_len), jnp.int32),
-            pltpu.VMEM((DEPTH, count), jnp.bfloat16),
-            pltpu.VMEM((16, width), jnp.float32),
-            pltpu.VMEM((GROUP, count), jnp.float32),
-            pltpu.VMEM((block_len // (GROUP * DEPTH), count), jnp.float32),
-            pltpu.VMEM((2 * RING, count), jnp.float32),
-            pltpu.VMEM((2 * GROUP * EX, DEPTH), jnp.bfloat16),
-            pltpu.VMEM((2, EX, count), jnp.float32),
-            pltpu.VMEM((2, BF - 1, RING, width), jnp.float32),
-            pltpu.VMEM((2, BF, RING, width), jnp.float32),
+            pltpu.VMEM((DEPTH, slot_count), jnp.bfloat16),
+            pltpu.VMEM((16, slotted), jnp.float32),
+            pltpu.VMEM((GROUP // 2, slot_count), jnp.float32),
+            pltpu.VMEM((block_len // (GROUP * DEPTH), slot_count), jnp.float32),
+            pltpu.VMEM((2 * RING, slot_count), jnp.float32),
+            pltpu.VMEM((2, GROUP * EX, DEPTH), jnp.bfloat16),
+            pltpu.VMEM((BF, width), jnp.int32),
+            pltpu.VMEM((LANES, width), jnp.bfloat16),
+            pltpu.SMEM((slot_count // TILE,), jnp.int32),
+            pltpu.VMEM((2, EX, slot_count), jnp.float32),
+            pltpu.VMEM((2, BF - 1, RING, slotted), jnp.float32),
+            pltpu.VMEM((2, BF, RING, slotted), jnp.float32),
             pltpu.VMEM((EX, width), jnp.float32),
             pltpu.VMEM((EX, width), jnp.float32),
             dma,

time: 45.7 us -> 43.2 us (0.945)
  Pallas kernels: 44.2 us -> 41.7 us
    pallas_call x1, Pallas kernels: 44.2 us -> 41.7 us  [per_device(): pl.pallas_call(kernel, out_shape=jax.ShapeDtypeStruct((1, width), jnp.flo...]
where the time goes in v5:
time: 43.2 us; the launch traced here: 43 us
  Pallas kernels  41.7 us (97%)
  local copies, waits for them, and re-layouts  1.28 us (3%)
    pallas_call x1, Pallas kernels, per_device(): pl.pallas_call(kernel, out_shape=jax.ShapeDtypeStruct((1, width), jnp.flo...  41.7 us
    unnamed x1, local copies, waits for them, and re-layouts  1.28 us

profile of v5, /device:TPU:1, one launch (start us, length us, event | category | flops | bytes accessed | tf_op | source)
XLA Modules:
  0.0 43.0 jit_solution(13505799421485857390)
XLA Ops:
  0.0 41.7 %shard_map.64 = f32[1,1024]{1,0:T(1,128)} custom-call(f32[16,32768]{1,0:T(8,128)} %bitcast.5, f32[1,32768]{1,0:T(1,128)} %bitcast.6, f32[1,32768]{1,0:T(1,128)} %bitcast.7, s32[1,32768]{1,0:T(1,128)} %bitcast.8, s32[1,8192]{1,0:T(1,128)} %bitcast.9, s32[16]{0:T(128)} %pool_ref.1), custom_call_target="tpu_custom_call" | custom-call | tf_op jit(solution)/shard_map/pallas_call | solution.py:336
  41.7 1.3 %copy.8 = f32[1,1024]{1,0:T(1,128)} copy(f32[1,1024]{1,0:T(1,128)} %shard_map.64) | data formatting | bytes 8192

commit v6 on v5

--- a/solution.py
+++ b/solution.py
@@ -39,15 +39,15 @@
 
 
 def kernel(
-    g_ref, one_ref, two_ref, flip_ref, rows_ref, pool_ref, out_ref,
-    recv, one, two, flip, weight, coarse, sign_low, sign_high, sign_row, left, slots, unsort, which, part, outbox, inbox, mine, got_ex,
-    g_send, g_recv, m_send, m_recv, bf_send, bf_recv, ex_send, ex_recv,
+    g_ref, one_ref, two_ref, flip_ref, rows_hbm, pool_hbm, out_ref,
+    rows_ref, pool_ref, recv, one, two, flip, weight, coarse, sign_low, sign_high, sign_row, left, slots, unsort, which, part, outbox, inbox, mine, got_ex,
+    g_send, g_recv, m_send, m_recv, bf_send, bf_recv, ex_send, ex_recv, local_sem,
 ):
     ex = lax.axis_index("ex")
     bf = lax.axis_index("bf")
     z, y = ex // RING, ex % RING
     block_len = g_ref.shape[1]
-    count = rows_ref.shape[1]
+    count = rows_hbm.shape[1]
     side_len = block_len // 2
     width = count // BF
     slotted = width + TILE
@@ -59,6 +59,9 @@
     def bf_peer(dx, flip_core):
         core = bf % 2
         return (bf // 2 + dx) % RING * 2 + (1 - core if flip_core else core)
+
+    samples = pltpu.make_async_copy(rows_hbm, rows_ref, local_sem.at[0])
+    pools = pltpu.make_async_copy(pool_hbm, pool_ref, local_sem.at[1])
 
     barrier = pltpu.get_barrier_semaphore()
     for d in (2, 1, 3):
@@ -66,6 +69,8 @@
         pl.semaphore_signal(barrier, inc=1, device_id=(owner(0, d), bf), device_id_type=MESH)
     for dx, flip_core in TILES:
         pl.semaphore_signal(barrier, inc=1, device_id=(ex, bf_peer(dx, flip_core)), device_id_type=MESH)
+    samples.start()
+    pools.start()
     pl.semaphore_wait(barrier, 2 * (RING - 1) + BF - 1)
 
     moments = ((one_ref, one), (two_ref, two), (flip_ref, flip))
@@ -114,6 +119,8 @@
     for number, (spans, first) in enumerate(order):
         send_chunk(number, spans, first)
 
+    samples.wait()
+    pools.wait()
     codes = jnp.concatenate([rows_ref[:, b * width : (b + 1) * width] for b in range(BF)], axis=0)
     bit = (codes >> 8) & 1
     before = lax.broadcasted_iota(jnp.int32, (LANES, LANES), 0) < lax.broadcasted_iota(jnp.int32, (LANES, LANES), 1)
@@ -335,11 +342,12 @@
     dma = pltpu.SemaphoreType.DMA
     return pl.pallas_call(
         kernel,
-        out_shape=jax.ShapeDtypeStruct((1, width), jnp.float32),
-        in_specs=[pl.BlockSpec(memory_space=pl.ANY)] * 4
-        + [pl.BlockSpec(memory_space=pltpu.VMEM), pl.BlockSpec(memory_space=pltpu.SMEM)],
+        out_shape=pltpu.VMEM((1, width), jnp.float32),
+        in_specs=[pl.BlockSpec(memory_space=pl.ANY)] * 6,
         out_specs=pl.BlockSpec(memory_space=pltpu.VMEM),
         scratch_shapes=[
+            pltpu.VMEM((1, count), jnp.int32),
+            pltpu.SMEM((EX,), jnp.int32),
             pltpu.VMEM((2, EX, side_len), jnp.float32),
             pltpu.VMEM((2, RING, side_len), jnp.float32),
             pltpu.VMEM((2, RING, side_len), jnp.float32),
@@ -366,6 +374,7 @@
             dma((2, BF - 1)),
             dma,
             dma,
+            dma((2,)),
         ],
         compiler_params=pltpu.CompilerParams(
             collective_id=0, has_side_effects=True, vmem_limit_bytes=56 * 2**20

time: 43.2 us -> 41.1 us (0.951)
  Pallas kernels: 41.7 us -> 40.4 us
  local copies, waits for them, and re-layouts: 1.28 us -> 0.6 us
    pallas_call x1, Pallas kernels: 41.7 us -> 40.4 us  [per_device(): pl.pallas_call(kernel, out_shape=pltpu.VMEM((1, width), jnp.float32), in_...]
    unnamed x1, local copies, waits for them, and re-layouts: 1.28 us -> 0.6 us
where the time goes in v6:
time: 41.1 us; the launch traced here: 41 us
  Pallas kernels  40.4 us (98%)
  local copies, waits for them, and re-layouts  0.6 us (1%)
    pallas_call x1, Pallas kernels, per_device(): pl.pallas_call(kernel, out_shape=pltpu.VMEM((1, width), jnp.float32), in_...  40.4 us

profile of v6, /device:TPU:1, one launch (start us, length us, event | category | flops | bytes accessed | tf_op | source)
XLA Modules:
  0.0 41.0 jit_solution(10532471573165534379)
XLA Ops:
  0.0 40.4 %shard_map.64 = f32[1,1024]{1,0:T(1,128)S(1)} custom-call(f32[16,32768]{1,0:T(8,128)} %bitcast.5, f32[1,32768]{1,0:T(1,128)} %bitcast.6, f32[1,32768]{1,0:T(1,128)} %bitcast.7, s32[1,32768]{1,0:T(1,128)} %bitcast.8, s32[1,8192]{1,0:T(1,128)} %bitcast.9, s32[16]{0:T(128)} %pool_hbm.1), custom_call_target="tpu_custom_call" | custom-call | tf_op jit(solution)/shard_map/pallas_call | solution.py:343
  40.4 0.6 %copy.8 = f32[1,1024]{1,0:T(1,128)} copy(f32[1,1024]{1,0:T(1,128)S(1)} %shard_map.64) | data formatting | bytes 8192

commit v7 on v6

--- a/solution.py
+++ b/solution.py
@@ -75,9 +75,9 @@
 
     moments = ((one_ref, one), (two_ref, two), (flip_ref, flip))
 
-    def send_chunk(number, spans, first):
+    def send_chunk(side, number, spans, first):
         size = spans * DEPTH
-        for side in (0, 1):
+        for _ in (0,):
             own, other = (y, z) if side == 0 else (z, y)
             source = pl.ds(side * side_len + first * DEPTH, size)
             place = pl.ds(first * DEPTH, size)
@@ -116,8 +116,8 @@
                     src.at[0, source], dst.at[side, other, place], m_recv.at[k, side, number]
                 ).start()
 
-    for number, (spans, first) in enumerate(order):
-        send_chunk(number, spans, first)
+    for side, number in [(0,0),(1,0),(0,1),(1,1),(0,2),(1,2),(0,3),(1,3),(0,4),(0,5),(1,4),(1,5)]:
+        send_chunk(side, number, *order[number])
 
     samples.wait()
     pools.wait()
@@ -172,7 +172,7 @@
         sign_row[:, place] = parity_sign((rows[:8] & row_mask) >> 18, 4)
         return carry
 
-    lax.fori_loop(0, BF, signs, 0, unroll=2)
+    lax.fori_loop(0, BF, signs, 0, unroll=8)
     unsort[...] = one_hot(slots[pl.ds(bf, 1), :])
     part[...] = jnp.zeros_like(part)
 
@@ -251,30 +251,39 @@
         )
 
     number, start = 0, 0
-    for spans, many in PLAN:
+    for spans, many in PLAN[:2]:
 
         def step_chunk(step, carry, spans=spans, number=number, start=start):
             do_chunk(step % 2, number + step // 2, spans, start + step // 2 * spans)
             return carry
 
-        steps = 2 * many - (2 if number + many == len(order) else 0)
-        lax.fori_loop(0, steps, step_chunk, 0)
+        lax.fori_loop(0, 2 * many, step_chunk, 0)
         number, start = number + many, start + many * spans
 
+    spans, many = PLAN[2]
+
+    def step_side(step, carry):
+        do_chunk(0, number + step, spans, start + step * spans)
+        return carry
+
+    lax.fori_loop(0, many, step_side, 0)
     number, (spans, first) = len(order) - 1, order[-1]
     tiles = [bf_peer(*peer) for peer in TILES] + [bf]
-    do_chunk(0, number, spans, first)
     for side in (0, 1):
         if side == 1:
+            do_chunk(side, number - 1, *order[number - 1])
             features(side, number, spans, first)
-        for slot, t in enumerate(tiles):
-            place = pl.ds(pl.multiple_of(t * slotted, slotted), slotted)
-            total = part[side, :, place] if side == 0 else tile(side, spans, first, t)
-            if slot < len(TILES):
-                outbox[side, slot] = by_example(side, total, place)
+        size = BF if side == 0 else 2
+        for begin in range(0, BF, size):
+            for slot in range(begin, begin + size):
+                place = pl.ds(pl.multiple_of(tiles[slot] * slotted, slotted), slotted)
+                total = part[side, :, place] if side == 0 else tile(side, spans, first, tiles[slot])
+                if slot < len(TILES):
+                    outbox[side, slot] = by_example(side, total, place)
+                else:
+                    inbox[side, slot] = by_example(side, total, place)
+            for slot in range(begin, min(begin + size, len(TILES))):
                 bf_copy(side, slot).start()
-            else:
-                inbox[side, slot] = by_example(side, total, place)
     summed = []
     for side in (0, 1):
         found = inbox[side, BF - 1]

time: 41.1 us -> 40.9 us (level)
  no operation moved by 1% of the time
where the time goes in v7:
time: 40.9 us; the launch traced here: 40.8 us
  Pallas kernels  40.2 us (98%)
  local copies, waits for them, and re-layouts  0.6 us (1%)
    pallas_call x1, Pallas kernels, per_device(): pl.pallas_call(kernel, out_shape=pltpu.VMEM((1, width), jnp.float32), in_...  40.2 us

profile of v7, /device:TPU:1, one launch (start us, length us, event | category | flops | bytes accessed | tf_op | source)
XLA Modules:
  0.0 40.8 jit_solution(5086374889271067933)
XLA Ops:
  0.0 40.2 %shard_map.64 = f32[1,1024]{1,0:T(1,128)S(1)} custom-call(f32[16,32768]{1,0:T(8,128)} %bitcast.5, f32[1,32768]{1,0:T(1,128)} %bitcast.6, f32[1,32768]{1,0:T(1,128)} %bitcast.7, s32[1,32768]{1,0:T(1,128)} %bitcast.8, s32[1,8192]{1,0:T(1,128)} %bitcast.9, s32[16]{0:T(128)} %pool_hbm.1), custom_call_target="tpu_custom_call" | custom-call | tf_op jit(solution)/shard_map/pallas_call | solution.py:352
  40.2 0.6 %copy.8 = f32[1,1024]{1,0:T(1,128)} copy(f32[1,1024]{1,0:T(1,128)S(1)} %shard_map.64) | data formatting | bytes 8192

commit v8 on v7

--- a/solution.py
+++ b/solution.py
@@ -294,14 +294,14 @@
 
     found = jnp.concatenate(summed, axis=0)
     terms = []
-    for _ in range(3):
+    for _ in range(2):
         term = found.astype(jnp.bfloat16).astype(jnp.float32)
         found = found - term
         terms += [term[:, i * LANES : (i + 1) * LANES] for i in range(slotted // LANES)]
     stacked = jnp.concatenate(terms, axis=0).astype(jnp.bfloat16)
     spread = jnp.dot(stacked, unsort[...], preferred_element_type=jnp.float32)
     size = slotted // LANES * 8
-    spread = spread[:size] + spread[size : 2 * size] + spread[2 * size :]
+    spread = spread[:size] + spread[size:]
     chosen = jnp.broadcast_to(slots[pl.ds(bf, 1), :] >> 7, (8, width))
     summed = jnp.zeros((8, width), jnp.float32)
     for i in range(slotted // LANES):

time: 40.9 us -> 40.8 us (level)
  no operation moved by 1% of the time
where the time goes in v8:
time: 40.8 us; the launch traced here: 40.7 us
  Pallas kernels  40.1 us (98%)
  local copies, waits for them, and re-layouts  0.6 us (1%)
    pallas_call x1, Pallas kernels, per_device(): pl.pallas_call(kernel, out_shape=pltpu.VMEM((1, width), jnp.float32), in_...  40.1 us

profile of v8, /device:TPU:1, one launch (start us, length us, event | category | flops | bytes accessed | tf_op | source)
XLA Modules:
  0.0 40.7 jit_solution(12384786424865445792)
XLA Ops:
  0.0 40.1 %shard_map.64 = f32[1,1024]{1,0:T(1,128)S(1)} custom-call(f32[16,32768]{1,0:T(8,128)} %bitcast.5, f32[1,32768]{1,0:T(1,128)} %bitcast.6, f32[1,32768]{1,0:T(1,128)} %bitcast.7, s32[1,32768]{1,0:T(1,128)} %bitcast.8, s32[1,8192]{1,0:T(1,128)} %bitcast.9, s32[16]{0:T(128)} %pool_hbm.1), custom_call_target="tpu_custom_call" | custom-call | tf_op jit(solution)/shard_map/pallas_call | solution.py:352
  40.1 0.6 %copy.8 = f32[1,1024]{1,0:T(1,128)} copy(f32[1,1024]{1,0:T(1,128)S(1)} %shard_map.64) | data formatting | bytes 8192
